TPU v7x, 32 devices: a whole 2x2x4 slice. The times are simulated.
32 devices in a mesh: tm: 4 (over y, x), lon: 8 (over z, core).
Axes of the slice: x: 2, y: 2, z: 4, core: 2. Of those that a mesh axis runs over, the one named last changes fastest.
Arguments:
- first_guess: float32 [8, 64, 80, 64], P('tm', 'lon'), may hold values from -6 to 6
- background: float32 [64, 80, 64], P('lon'), may hold values from -6 to 6
- opening_kernel_matrix: bfloat16 [256, 720], replicated, may hold values from -0.21875 to 0.21875
- hidden_layer_shift: float32 [256], replicated, may hold values from -3 to 3
- closing_kernel_matrix: bfloat16 [80, 2304], replicated, may hold values from -0.125 to 0.125
- output_layer_shift: float32 [80], replicated, may hold values from -2 to 2
- model_weight: float32 [80], replicated, may hold values from 0.5 to 2
- background_weight: float32 [80], replicated, may hold values from 0.5 to 2
- obs_cell: int32 [8, 2048], P('tm', 'lon'), may hold values from 0 to 511
- obs_chan: int32 [8, 2048], P('tm', 'lon'), may hold values from 0 to 79
- obs_value: float32 [8, 2048], P('tm', 'lon'), may hold values from -6 to 6
- obs_weight: float32 [8, 2048], P('tm', 'lon'), may hold values from 0.5 to 4
- step_size: float32 [], replicated, may hold values from 0.3 to 0.6
Outputs:
- analysis: float32 [8, 64, 80, 64], P('tm', 'lon')
- costs: float32 [2], replicated
Inputs may be any that keep to these rules, and one draw needn't show every extreme that they name: `obs_cell`: the band of an observation is its column block of 256; the value counts cells of that band, longitude-major.
All inputs are finite; a program needn't handle non-finite values.
Results may differ from a plain program's by a relative error of at most 0.0085.
Values may be sent and summed in bfloat16 or wider, within the bound.
A program may use at most 64 MiB of HBM per device.

v0:
```python
import jax
import jax.numpy as jnp
from jax import lax
from jax.sharding import PartitionSpec as P

ITERS = 2


def padded_2(cells, sides, width):
    for axis, dim in sides:
        count = lax.axis_size(axis)
        head = lax.slice_in_dim(cells, 0, width, axis=dim)
        tail = lax.slice_in_dim(cells, cells.shape[dim] - width, cells.shape[dim], axis=dim)
        cells = jnp.concatenate(
            [
                lax.ppermute(tail, axis, [(i, (i + 1) % count) for i in range(count)]),
                cells,
                lax.ppermute(head, axis, [((i + 1) % count, i) for i in range(count)]),
            ],
            axis=dim,
        )
    return cells


def for_sending(value):
    return jax.tree.map(lambda a: a.astype(jnp.bfloat16) if a.dtype == jnp.float32 else a, value)


def passed_along(value, axis, by):
    length = lax.axis_size(axis)
    pairs = [(i, i + by) for i in range(length) if 0 <= i + by < length]
    return lax.ppermute(value, axis, pairs)


def adjoint_weight(weight):
    rows_out = weight.shape[0]
    rows_in = weight.shape[1] // 9
    flipped = weight.reshape(rows_out, 3, 3, rows_in)[:, ::-1, ::-1, :]
    return flipped.transpose(3, 1, 2, 0).reshape(rows_in, 9 * rows_out)


def convolve(padded, weight):
    count = padded.shape[1] - 2
    lats = padded.shape[3]
    spread = jnp.pad(padded, ((0, 0), (0, 0), (0, 0), (1, 1)))
    stacked = jnp.concatenate(
        [spread[:, a : a + count, :, b : b + lats] for a in range(3) for b in range(3)], axis=2
    )
    return jnp.einsum("fk,snkl->snfl", weight, stacked, preferred_element_type=jnp.float32)


def propagate_onestep(
    system_vector,
    opening_kernel_matrix,
    opening_offset_vector,
    closing_kernel_matrix,
    closing_offset_vector,
):
    lowered = system_vector.astype(jnp.bfloat16)
    padded_state = padded_2(lowered, (("lon", 1),), 2)
    nonlinear_argument = convolve(padded_state, opening_kernel_matrix) + opening_offset_vector
    hidden = jax.nn.gelu(nonlinear_argument).astype(jnp.bfloat16)
    output = convolve(hidden, closing_kernel_matrix)
    return (system_vector + output + closing_offset_vector, nonlinear_argument)


def pullback(cotangent, nonlinear_argument, w_in_adj, w_out_adj):
    lowered = cotangent.astype(jnp.bfloat16)
    padded_cot = padded_2(lowered, (("lon", 1),), 2)
    inner = convolve(padded_cot, w_out_adj)
    scaled_wide = jax.vjp(jax.nn.gelu, nonlinear_argument)[1](inner)[0].astype(jnp.bfloat16)
    return cotangent + convolve(scaled_wide, w_in_adj)


def per_device(
    first_guess,
    background,
    opening_kernel_matrix,
    hidden_layer_shift,
    closing_kernel_matrix,
    output_layer_shift,
    model_weight,
    background_weight,
    obs_cell,
    obs_chan,
    obs_value,
    obs_weight,
    step_size,
):
    subs, band, chans, lats = first_guess.shape
    place = lax.axis_index("tm")
    total = float(subs * lax.axis_size("tm") * band * lax.axis_size("lon") * chans * lats)
    w_in_adj = adjoint_weight(opening_kernel_matrix)
    w_out_adj = adjoint_weight(closing_kernel_matrix)
    opening_offset_vector = hidden_layer_shift[None, None, :, None]
    closing_offset_vector = output_layer_shift[None, None, :, None]
    model_scale = model_weight[None, None, :, None]
    back_scale = background_weight[None, None, :, None]
    flat = obs_cell // lats * (chans * lats) + obs_chan * lats + obs_cell % lats
    rows = jnp.broadcast_to(jnp.arange(subs, dtype=jnp.int32)[:, None], flat.shape)
    local = jnp.arange(subs)
    starts = ((local > 0) | (place > 0)).astype(jnp.float32)[:, None, None, None]
    anchor = ((local == 0) & (place == 0)).astype(jnp.float32)[:, None, None, None]
    system_vector = first_guess
    costs = []
    for step in range(ITERS):
        propagate_trajectory, nonlinear_argument = propagate_onestep(
            system_vector,
            opening_kernel_matrix,
            opening_offset_vector,
            closing_kernel_matrix,
            closing_offset_vector,
        )
        incoming_vector = passed_along(for_sending(propagate_trajectory[-1]), "tm", 1)
        earlier_iterate = jnp.concatenate(
            [incoming_vector[None], propagate_trajectory[:-1]], axis=0
        )
        defect = system_vector - earlier_iterate
        forcing = model_scale * defect * starts
        returned = passed_along(for_sending(forcing[0]), "tm", -1)
        later = jnp.concatenate([forcing[1:], returned[None]], axis=0)
        pulled = pullback(later, nonlinear_argument, w_in_adj, w_out_adj)
        estimate = jnp.take_along_axis(system_vector.reshape(subs, -1), flat, axis=1)
        misfit = estimate - obs_value
        weighted = obs_weight * misfit
        observed = (
            jnp.zeros((subs, band * chans * lats), jnp.float32)
            .at[rows, flat]
            .add(weighted)
            .reshape(system_vector.shape)
        )
        departure = (system_vector - background[None]) * anchor
        gradient = forcing - pulled + observed + back_scale * departure
        partial_cost = 0.5 * (
            jnp.sum(forcing * defect)
            + jnp.sum(weighted * misfit)
            + jnp.sum(back_scale * departure * departure)
        )
        squares = jnp.sum(gradient * gradient)
        cost = lax.psum(partial_cost, ("tm", "lon"))
        norm = lax.psum(squares, ("tm", "lon"))
        costs.append(cost)
        system_vector = system_vector - step_size / jnp.sqrt(norm / total + 1e-06) * gradient
    return (system_vector, jnp.stack(costs))


def solution(mesh):
    in_specs = (
        P("tm", "lon", None, None),
        P("lon", None, None),
        P(),
        P(),
        P(),
        P(),
        P(),
        P(),
        P("tm", "lon"),
        P("tm", "lon"),
        P("tm", "lon"),
        P("tm", "lon"),
        P(),
    )
    out_specs = (P("tm", "lon", None, None), P())
    return jax.shard_map(
        per_device, mesh=mesh, in_specs=in_specs, out_specs=out_specs, check_vma=False
    )
```

profile of v0, /device:TPU:0, one launch (start us, length us, event | category | flops | bytes accessed | tf_op | source)
XLA Modules:
  0.0 261.3 jit_solution(857331586531488549)
XLA Ops:
  0.6 1.1 convert_element_type.88
  2.3 4.1 %collective-permute-start.1 = (bf16[2,2,80,64]{2,3,1,0:T(8,128)(2,1)S(1)}, bf16[2,2,80,64]{2,3,1,0:T(8,128)(2,1)S(1)}, u32[]{:S(2)}, u32[]{:S(2)}) collective-permute-start(bf16[2,2,80,64]{2,3,1,0:T(8,128)(2,1)S(1)} %get-tuple-element.64), channel_id=1, source_target_pairs={{1,0},{2,1},{3,2},{4,3},{5,4},{6,5},{7,6},{0,7},{9,8},{10,9},{11,1... | collective-permute-start | bytes 122888 | tf_op jit(solution)/shard_map/ppermute | solution.py:18
  6.4 1.3 copy.24
  8.7 4.8 %gather_fusion = f32[512]{0:T(512)S(1)} fusion(f32[2,40960]{1,0:T(2,128)S(1)} %reshape.81, s32[512]{0:T(512)S(1)} %bitcast.136), kind=kCustom, calls=%fused_computation.clone | custom fusion | bytes 8192 | tf_op jit(solution)/shard_map/jit(take_along_axis)/gather | solution.py:123
  13.8 1.7 pad_maximum_fusion.7
  15.5 3.8 %concatenate.79 = bf16[2,10,720,64]{2,3,1,0:T(8,128)(2,1)S(1)} concatenate(bf16[2,10,80,64]{2,3,1,0:T(8,128)(2,1)S(1)} %get-tuple-element.74, bf16[2,10,80,64]{2,3,1,0:T(8,128)(2,1)S(1)} %get-tuple-element.62, bf16[2,10,80,64]{2,3,1,0:T(8,128)(2,1)} %get-tuple-element.79, bf16[2,10,80,64]{2,3,1,0:T(8,128)(2,1)} %get-tuple-element.78, bf16[2,10,80,64]{2,3,1,0:T(8,128)(2,1)} %get-tuple-element.75, ...), dimensions={2} | concatenate | bytes 3686400 | tf_op jit(solution)/shard_map/concatenate | solution.py:46
  19.3 2.9 %multiply_convert_fusion.1 = (bf16[2,10,256,64]{2,3,1,0:T(8,128)(2,1)S(1)}, f32[2,10,256,64]{2,3,1,0:T(8,128)}) fusion(f32[256]{0:T(256)S(1)} %copy-done.17, bf16[2,10,720,64]{2,3,1,0:T(8,128)(2,1)S(1)} %concatenate.79, bf16[256,720]{0,1:T(8,128)(2,1)} %param.17), kind=kOutput, calls=%fused_computation.29 | convolution fusion | flops 475136000 | bytes 4178944 | tf_op jit(solution)/shard_map/fk,snkl->snfl/dot_general | solution.py:49
  23.5 1.4 fusion.23
  24.9 3.8 %collective-permute-start.2 = (bf16[8,80,64]{1,2,0:T(8,128)(2,1)S(1)}, bf16[8,80,64]{1,2,0:T(8,128)(2,1)S(1)}, u32[]{:S(2)}, u32[]{:S(2)}) collective-permute-start(bf16[8,80,64]{1,2,0:T(8,128)(2,1)S(1)} %fusion.38), channel_id=1, source_target_pairs={{0,8},{8,16},{16,24},{1,9},{9,17},{17,25},{2,10},{10,18},{18,26},{... | collective-permute-start | bytes 245768 | tf_op jit(solution)/shard_map/ppermute | solution.py:32
  28.8 2.5 collective-permute-done.2
  31.5 1.3 collective-permute-start.3
  32.9 5.9 %collective-permute-done.3 = bf16[8,80,64]{1,2,0:T(8,128)(2,1)S(1)} collective-permute-done((bf16[8,80,64]{1,2,0:T(8,128)(2,1)S(1)}, bf16[8,80,64]{1,2,0:T(8,128)(2,1)S(1)}, u32[]{:S(2)}, u32[]{:S(2)}) %collective-permute-start.3) | collective-permute-done | bytes 81952 | tf_op jit(solution)/shard_map/ppermute | solution.py:32
  39.0 3.5 %collective-permute-start.5 = (bf16[2,2,80,64]{2,3,1,0:T(8,128)(2,1)S(1)}, bf16[2,2,80,64]{2,3,1,0:T(8,128)(2,1)S(1)}, u32[]{:S(2)}, u32[]{:S(2)}) collective-permute-start(bf16[2,2,80,64]{2,3,1,0:T(8,128)(2,1)S(1)} %get-tuple-element.60), channel_id=1, source_target_pairs={{1,0},{2,1},{3,2},{4,3},{5,4},{6,5},{7,6},{0,7},{9,8},{10,9},{11,1... | collective-permute-start | bytes 122888 | tf_op jit(solution)/shard_map/ppermute | solution.py:18
  42.5 0.9 reshape.77
  43.4 3.3 %rev.6 = bf16[80,3,3,256]{3,2,1,0:T(4,128)(2,1)S(1)} reverse(bf16[80,3,3,256]{3,2,1,0:T(4,128)(2,1)} %reshape.77), dimensions={1,2} | reverse | bytes 737280 | tf_op jit(solution)/shard_map/rev | solution.py:38
  47.6 23.6 %scatter_fusion = f32[2,40960]{1,0:T(2,128)S(1)} fusion(f32[2,40960]{1,0:T(2,128)S(1)} %broadcast.105.clone, s32[512]{0:T(512)S(1)} %bitcast.134, f32[512]{0:T(512)S(1)} %bitcast.143), kind=kCustom, calls=%fused_computation.2 | custom fusion | flops 512 | bytes 10240 | tf_op jit(solution)/shard_map/scatter-add | solution.py:129
  71.6 1.0 copy.25
  72.7 2.0 copy.23
  74.7 3.3 %rev.7 = bf16[256,3,3,80]{0,2,1,3:T(4,128)(2,1)S(1)} reverse(bf16[256,3,3,80]{0,2,1,3:T(4,128)(2,1)} %copy.23), dimensions={1,2} | reverse | bytes 737280 | tf_op jit(solution)/shard_map/rev | solution.py:38
  79.2 1.4 pad_slice_fusion.12
  80.6 1.0 pad_maximum_fusion.9
  81.6 5.0 %concatenate.86 = bf16[2,10,720,64]{2,3,1,0:T(8,128)(2,1)} concatenate(bf16[2,10,80,64]{2,3,1,0:T(8,128)(2,1)} %get-tuple-element.41, bf16[2,10,80,64]{2,3,1,0:T(8,128)(2,1)} %get-tuple-element.58, bf16[2,10,80,64]{2,3,1,0:T(8,128)(2,1)S(1)} %get-tuple-element.36, bf16[2,10,80,64]{2,3,1,0:T(8,128)(2,1)} %get-tuple-element.37, bf16[2,10,80,64]{2,3,1,0:T(8,128)(2,1)} %get-tuple-element.40, ...), dimensions={2} | concatenate | bytes 3686400 | tf_op jit(solution)/shard_map/concatenate | solution.py:46
  86.6 3.2 %fusion.8 = bf16[2,10,256,64]{2,3,1,0:T(8,128)(2,1)S(1)} fusion(f32[2,10,256,64]{2,3,1,0:T(8,128)} %get-tuple-element.67, bf16[2,10,720,64]{2,3,1,0:T(8,128)(2,1)} %concatenate.86, bf16[256,720,1,1]{0,1,3,2:T(8,128)(2,1)} %bitcast.141), kind=kOutput, calls=%fused_computation.20 | convolution fusion | flops 478412800 | bytes 4177920 | tf_op jit(solution)/shard_map/fk,snkl->snfl/dot_general | solution.py:49
  91.1 2.1 multiply_reduce_fusion.3
  93.2 38.0 %psum.28 = f32[]{:T(128)} all-reduce(f32[]{:T(128)} %get-tuple-element.68), channel_id=1, replica_groups=mesh['tm'=4,'lon'=8] {'tm','lon'}, use_global_device_ids=true, to_apply=%region_2.4 | all-reduce | flops 1 | bytes 8 | tf_op jit(solution)/shard_map/psum | solution.py:141
  132.1 3.5 %collective-permute-start.7 = (bf16[2,2,80,64]{2,3,1,0:T(8,128)(2,1)S(1)}, bf16[2,2,80,64]{2,3,1,0:T(8,128)(2,1)S(1)}, u32[]{:S(2)}, u32[]{:S(2)}) collective-permute-start(bf16[2,2,80,64]{2,3,1,0:T(8,128)(2,1)S(1)} %get-tuple-element.56), channel_id=1, source_target_pairs={{1,0},{2,1},{3,2},{4,3},{5,4},{6,5},{7,6},{0,7},{9,8},{10,9},{11,1... | collective-permute-start | bytes 122888 | tf_op jit(solution)/shard_map/ppermute | solution.py:18
  135.6 1.9 collective-permute-done.6
  137.7 1.4 pad_slice_fusion.6
  139.0 0.9 pad_maximum_fusion.11
  140.0 5.0 %concatenate.92 = bf16[2,10,720,64]{2,3,1,0:T(8,128)(2,1)} concatenate(bf16[2,10,80,64]{2,3,1,0:T(8,128)(2,1)} %get-tuple-element.34, bf16[2,10,80,64]{2,3,1,0:T(8,128)(2,1)} %get-tuple-element.54, bf16[2,10,80,64]{2,3,1,0:T(8,128)(2,1)S(1)} %get-tuple-element.29, bf16[2,10,80,64]{2,3,1,0:T(8,128)(2,1)} %get-tuple-element.30, bf16[2,10,80,64]{2,3,1,0:T(8,128)(2,1)} %get-tuple-element.33, ...), dimensions={2} | concatenate | bytes 3686400 | tf_op jit(solution)/shard_map/concatenate | solution.py:46
  144.9 3.5 %multiply_convert_fusion = (bf16[2,10,256,64]{2,3,1,0:T(8,128)(2,1)S(1)}, f32[2,10,256,64]{2,3,1,0:T(8,128)}) fusion(f32[256]{0:T(256)S(1)} %copy-done.17, bf16[2,10,720,64]{2,3,1,0:T(8,128)(2,1)} %concatenate.92, bf16[256,720]{0,1:T(8,128)(2,1)} %param.17), kind=kOutput, calls=%fused_computation.28 | convolution fusion | flops 475136000 | bytes 4178944 | tf_op jit(solution)/shard_map/fk,snkl->snfl/dot_general | solution.py:49
  149.6 1.4 fusion.19
  151.0 4.2 %collective-permute-start.8 = (bf16[8,80,64]{1,2,0:T(8,128)(2,1)S(1)}, bf16[8,80,64]{1,2,0:T(8,128)(2,1)S(1)}, u32[]{:S(2)}, u32[]{:S(2)}) collective-permute-start(bf16[8,80,64]{1,2,0:T(8,128)(2,1)S(1)} %fusion.40), channel_id=1, source_target_pairs={{0,8},{8,16},{16,24},{1,9},{9,17},{17,25},{2,10},{10,18},{18,26},{... | collective-permute-start | bytes 245768 | tf_op jit(solution)/shard_map/ppermute | solution.py:32
  155.2 3.6 %collective-permute-done.8 = bf16[8,80,64]{1,2,0:T(8,128)(2,1)S(1)} collective-permute-done((bf16[8,80,64]{1,2,0:T(8,128)(2,1)S(1)}, bf16[8,80,64]{1,2,0:T(8,128)(2,1)S(1)}, u32[]{:S(2)}, u32[]{:S(2)}) %collective-permute-start.8) | collective-permute-done | bytes 81952 | tf_op jit(solution)/shard_map/ppermute | solution.py:32
  158.9 1.2 fusion.29
  160.2 1.3 collective-permute-start.9
  162.1 4.8 %gather_fusion.1 = f32[512]{0:T(512)S(1)} fusion(f32[2,40960]{1,0:T(2,128)S(1)} %reshape.83, s32[512]{0:T(512)S(1)} %bitcast.137), kind=kCustom, calls=%fused_computation.1.clone | custom fusion | bytes 8192 | tf_op jit(solution)/shard_map/jit(take_along_axis)/gather | solution.py:123
  166.9 1.4 collective-permute-done.9
  168.5 3.5 %collective-permute-start.11 = (bf16[2,2,80,64]{2,3,1,0:T(8,128)(2,1)S(1)}, bf16[2,2,80,64]{2,3,1,0:T(8,128)(2,1)S(1)}, u32[]{:S(2)}, u32[]{:S(2)}) collective-permute-start(bf16[2,2,80,64]{2,3,1,0:T(8,128)(2,1)S(1)} %get-tuple-element.52), channel_id=1, source_target_pairs={{1,0},{2,1},{3,2},{4,3},{5,4},{6,5},{7,6},{0,7},{9,8},{10,9},{11,1... | collective-permute-start | bytes 122888 | tf_op jit(solution)/shard_map/ppermute | solution.py:18
  172.7 23.6 %scatter_fusion.1 = f32[2,40960]{1,0:T(2,128)S(1)} fusion(f32[2,40960]{1,0:T(2,128)S(1)} %broadcast.105, s32[512]{0:T(512)S(1)} %bitcast.135, f32[512]{0:T(512)S(1)} %bitcast.144), kind=kCustom, calls=%fused_computation.3 | custom fusion | flops 512 | bytes 10240 | tf_op jit(solution)/shard_map/scatter-add | solution.py:129
  202.2 1.4 pad_slice_fusion
  203.5 1.8 pad_maximum_fusion.13
  205.3 4.7 %concatenate.99 = bf16[2,10,720,64]{2,3,1,0:T(8,128)(2,1)} concatenate(bf16[2,10,80,64]{2,3,1,0:T(8,128)(2,1)} %get-tuple-element.27, bf16[2,10,80,64]{2,3,1,0:T(8,128)(2,1)} %get-tuple-element.50, bf16[2,10,80,64]{2,3,1,0:T(8,128)(2,1)S(1)} %get-tuple-element.22, bf16[2,10,80,64]{2,3,1,0:T(8,128)(2,1)S(1)} %get-tuple-element.23, bf16[2,10,80,64]{2,3,1,0:T(8,128)(2,1)} %get-tuple-element.26, ...), dimensions={2} | concatenate | bytes 3686400 | tf_op jit(solution)/shard_map/concatenate | solution.py:46
  210.0 3.2 %fusion.15 = bf16[2,10,256,64]{2,3,1,0:T(8,128)(2,1)S(1)} fusion(f32[2,10,256,64]{2,3,1,0:T(8,128)} %get-tuple-element.71, bf16[2,10,720,64]{2,3,1,0:T(8,128)(2,1)} %concatenate.99, bf16[256,720,1,1]{0,1,3,2:T(8,128)(2,1)} %bitcast.142), kind=kOutput, calls=%fused_computation.27 | convolution fusion | flops 478412800 | bytes 4177920 | tf_op jit(solution)/shard_map/fk,snkl->snfl/dot_general | solution.py:49
  214.5 2.1 multiply_reduce_fusion.2
  216.6 41.2 %all-reduce.8 = (f32[]{:T(128)}, f32[1]{0:T(128)}, f32[1]{0:T(128)}) all-reduce(f32[]{:T(128)} %get-tuple-element.72, f32[1]{0:T(128)} %bitcast.35, f32[1]{0:T(128)} %bitcast.34), channel_id=1, replica_groups=mesh['tm'=4,'lon'=8] {'tm','lon'}, use_global_device_ids=true, to_apply=%region_5.7 | all-reduce | flops 3 | bytes 24 | tf_op jit(solution)/shard_map/psum | solution.py:141
  258.5 1.9 pad_maximum_fusion.14
  260.4 0.9 multiply_subtract_fusion
  (129 shorter events, 12.4 us)
Async XLA Ops:
  0.6 13.0 %copy-start.16 = (f32[2,256]{1,0:T(2,128)S(1)}, f32[2,256]{1,0:T(2,128)}, u32[]{:S(2)}) copy-start(f32[2,256]{1,0:T(2,128)} %param.25) | copy-start | bytes 6148
  0.6 13.0 %copy-start.15 = (f32[2,256]{1,0:T(2,128)S(1)}, f32[2,256]{1,0:T(2,128)}, u32[]{:S(2)}) copy-start(f32[2,256]{1,0:T(2,128)} %param.26) | copy-start | bytes 6148
  1.8 11.9 %collective-permute-start = (bf16[2,2,80,64]{2,3,1,0:T(8,128)(2,1)S(1)}, bf16[2,2,80,64]{2,3,1,0:T(8,128)(2,1)S(1)}, u32[]{:S(2)}, u32[]{:S(2)}) collective-permute-start(bf16[2,2,80,64]{2,3,1,0:T(8,128)(2,1)S(1)} %get-tuple-element.63), channel_id=1, source_target_pairs={{0,1},{1,2},{2,3},{3,4},{4,5},{5,6},{6,7},{7,0},{8,9},{9,10},{10,1... | collective-permute-start | bytes 122888 | tf_op jit(solution)/shard_map/ppermute | solution.py:16
  2.3 11.4 %collective-permute-start.1 = (bf16[2,2,80,64]{2,3,1,0:T(8,128)(2,1)S(1)}, bf16[2,2,80,64]{2,3,1,0:T(8,128)(2,1)S(1)}, u32[]{:S(2)}, u32[]{:S(2)}) collective-permute-start(bf16[2,2,80,64]{2,3,1,0:T(8,128)(2,1)S(1)} %get-tuple-element.64), channel_id=1, source_target_pairs={{1,0},{2,1},{3,2},{4,3},{5,4},{6,5},{7,6},{0,7},{9,8},{10,9},{11,1... | collective-permute-start | bytes 122888 | tf_op jit(solution)/shard_map/ppermute | solution.py:18
  13.6 5.6 %copy-start.17 = (f32[256]{0:T(256)S(1)}, f32[256]{0:T(256)}, u32[]{:S(2)}) copy-start(f32[256]{0:T(256)} %param.18) | copy-start | bytes 3076
  22.3 1.1 copy-start
  22.4 1.1 copy-start.2
  22.4 1.1 copy-start.14
  23.2 8.1 %copy-start.12 = (f32[80]{0:T(128)S(1)}, f32[80]{0:T(128)}, u32[]{:S(2)}) copy-start(f32[80]{0:T(128)} %param.21) | copy-start | bytes 964
  24.9 6.3 %collective-permute-start.2 = (bf16[8,80,64]{1,2,0:T(8,128)(2,1)S(1)}, bf16[8,80,64]{1,2,0:T(8,128)(2,1)S(1)}, u32[]{:S(2)}, u32[]{:S(2)}) collective-permute-start(bf16[8,80,64]{1,2,0:T(8,128)(2,1)S(1)} %fusion.38), channel_id=1, source_target_pairs={{0,8},{8,16},{16,24},{1,9},{9,17},{17,25},{2,10},{10,18},{18,26},{... | collective-permute-start | bytes 245768 | tf_op jit(solution)/shard_map/ppermute | solution.py:32
  31.5 7.3 %collective-permute-start.3 = (bf16[8,80,64]{1,2,0:T(8,128)(2,1)S(1)}, bf16[8,80,64]{1,2,0:T(8,128)(2,1)S(1)}, u32[]{:S(2)}, u32[]{:S(2)}) collective-permute-start(bf16[8,80,64]{1,2,0:T(8,128)(2,1)S(1)} %fusion.39), channel_id=1, source_target_pairs={{8,0},{16,8},{24,16},{9,1},{17,9},{25,17},{10,2},{18,10},{26,18},{... | collective-permute-start | bytes 245768 | tf_op jit(solution)/shard_map/ppermute | solution.py:32
  38.9 40.2 %collective-permute-start.4 = (bf16[2,2,80,64]{2,3,1,0:T(8,128)(2,1)S(1)}, bf16[2,2,80,64]{2,3,1,0:T(8,128)(2,1)S(1)}, u32[]{:S(2)}, u32[]{:S(2)}) collective-permute-start(bf16[2,2,80,64]{2,3,1,0:T(8,128)(2,1)S(1)} %get-tuple-element.59), channel_id=1, source_target_pairs={{0,1},{1,2},{2,3},{3,4},{4,5},{5,6},{6,7},{7,0},{8,9},{9,10},{10,1... | collective-permute-start | bytes 122888 | tf_op jit(solution)/shard_map/ppermute | solution.py:16
  39.0 40.1 %collective-permute-start.5 = (bf16[2,2,80,64]{2,3,1,0:T(8,128)(2,1)S(1)}, bf16[2,2,80,64]{2,3,1,0:T(8,128)(2,1)S(1)}, u32[]{:S(2)}, u32[]{:S(2)}) collective-permute-start(bf16[2,2,80,64]{2,3,1,0:T(8,128)(2,1)S(1)} %get-tuple-element.60), channel_id=1, source_target_pairs={{1,0},{2,1},{3,2},{4,3},{5,4},{6,5},{7,6},{0,7},{9,8},{10,9},{11,1... | collective-permute-start | bytes 122888 | tf_op jit(solution)/shard_map/ppermute | solution.py:18
  90.0 1.1 copy-start.1
  90.0 1.1 copy-start.9
  90.0 1.1 copy-start.13
  132.0 5.5 %collective-permute-start.6 = (bf16[2,2,80,64]{2,3,1,0:T(8,128)(2,1)S(1)}, bf16[2,2,80,64]{2,3,1,0:T(8,128)(2,1)S(1)}, u32[]{:S(2)}, u32[]{:S(2)}) collective-permute-start(bf16[2,2,80,64]{2,3,1,0:T(8,128)(2,1)S(1)} %get-tuple-element.55), channel_id=1, source_target_pairs={{0,1},{1,2},{2,3},{3,4},{4,5},{5,6},{6,7},{7,0},{8,9},{9,10},{10,1... | collective-permute-start | bytes 122888 | tf_op jit(solution)/shard_map/ppermute | solution.py:16
  132.1 5.5 %collective-permute-start.7 = (bf16[2,2,80,64]{2,3,1,0:T(8,128)(2,1)S(1)}, bf16[2,2,80,64]{2,3,1,0:T(8,128)(2,1)S(1)}, u32[]{:S(2)}, u32[]{:S(2)}) collective-permute-start(bf16[2,2,80,64]{2,3,1,0:T(8,128)(2,1)S(1)} %get-tuple-element.56), channel_id=1, source_target_pairs={{1,0},{2,1},{3,2},{4,3},{5,4},{6,5},{7,6},{0,7},{9,8},{10,9},{11,1... | collective-permute-start | bytes 122888 | tf_op jit(solution)/shard_map/ppermute | solution.py:18
  151.0 7.9 %collective-permute-start.8 = (bf16[8,80,64]{1,2,0:T(8,128)(2,1)S(1)}, bf16[8,80,64]{1,2,0:T(8,128)(2,1)S(1)}, u32[]{:S(2)}, u32[]{:S(2)}) collective-permute-start(bf16[8,80,64]{1,2,0:T(8,128)(2,1)S(1)} %fusion.40), channel_id=1, source_target_pairs={{0,8},{8,16},{16,24},{1,9},{9,17},{17,25},{2,10},{10,18},{18,26},{... | collective-permute-start | bytes 245768 | tf_op jit(solution)/shard_map/ppermute | solution.py:32
  155.2 4.9 %copy-start.5 = (f32[1,8,80,64]{2,3,1,0:T(8,128)}, f32[1,8,80,64]{2,3,1,0:T(8,128)S(1)}, u32[]{:S(2)}) copy-start(f32[1,8,80,64]{2,3,1,0:T(8,128)S(1)} %slice.395) | copy-start | bytes 491524
  158.9 1.3 copy-start.7
  160.2 8.2 %collective-permute-start.9 = (bf16[8,80,64]{1,2,0:T(8,128)(2,1)S(1)}, bf16[8,80,64]{1,2,0:T(8,128)(2,1)S(1)}, u32[]{:S(2)}, u32[]{:S(2)}) collective-permute-start(bf16[8,80,64]{1,2,0:T(8,128)(2,1)S(1)} %fusion.41), channel_id=1, source_target_pairs={{8,0},{16,8},{24,16},{9,1},{17,9},{25,17},{10,2},{18,10},{26,18},{... | collective-permute-start | bytes 245768 | tf_op jit(solution)/shard_map/ppermute | solution.py:32
  168.3 4.3 %copy-start.3 = (f32[1,8,80,64]{2,3,1,0:T(8,128)}, f32[1,8,80,64]{2,3,1,0:T(8,128)S(1)}, u32[]{:S(2)}) copy-start(f32[1,8,80,64]{2,3,1,0:T(8,128)S(1)} %bitcast_convert_fusion) | copy-start | bytes 491524
  168.4 32.4 %collective-permute-start.10 = (bf16[2,2,80,64]{2,3,1,0:T(8,128)(2,1)S(1)}, bf16[2,2,80,64]{2,3,1,0:T(8,128)(2,1)S(1)}, u32[]{:S(2)}, u32[]{:S(2)}) collective-permute-start(bf16[2,2,80,64]{2,3,1,0:T(8,128)(2,1)S(1)} %get-tuple-element.51), channel_id=1, source_target_pairs={{0,1},{1,2},{2,3},{3,4},{4,5},{5,6},{6,7},{7,0},{8,9},{9,10},{10,1... | collective-permute-start | bytes 122888 | tf_op jit(solution)/shard_map/ppermute | solution.py:16
  168.5 32.3 %collective-permute-start.11 = (bf16[2,2,80,64]{2,3,1,0:T(8,128)(2,1)S(1)}, bf16[2,2,80,64]{2,3,1,0:T(8,128)(2,1)S(1)}, u32[]{:S(2)}, u32[]{:S(2)}) collective-permute-start(bf16[2,2,80,64]{2,3,1,0:T(8,128)(2,1)S(1)} %get-tuple-element.52), channel_id=1, source_target_pairs={{1,0},{2,1},{3,2},{4,3},{5,4},{6,5},{7,6},{0,7},{9,8},{10,9},{11,1... | collective-permute-start | bytes 122888 | tf_op jit(solution)/shard_map/ppermute | solution.py:18
  200.8 0.6 copy-start.10
  201.5 0.6 copy-start.11
  213.4 1.1 copy-start.4
  213.4 1.1 copy-start.6
  213.5 1.1 copy-start.8
where the time goes:
time: 264 us; the launch traced here: 261 us
  blocking collectives  79.2 us (30%)
  other arithmetic  59.8 us (23%)
  local copies, waits for them, and re-layouts  53.7 us (20%)
  starting transfers between devices  26 us (10%)
  matrix products  19.8 us (8%)
  waiting for transfers between devices  15.4 us (6%)
  between operations  7.42 us (3%)
    psum x2, blocking collectives, per_device(): norm = lax.psum(squares, ('tm', 'lon'))  79.2 us
    scatter-add x2, other arithmetic, per_device(): observed = jnp.zeros((subs, band * chans * lats), jnp.float32).at[rows, f...  47.2 us
    dot_general x8, matrix products, convolve(): jnp.einsum('fk,snkl->snfl', weight, stacked, preferred_element_type=jnp.f...  19.8 us
    concatenate x8, local copies, waits for them, and re-layouts, convolve(): jnp.concatenate([spread[:, a:a + count, :, b:b + lats] for a in range(3)...  19.1 us
    ppermute x4, starting transfers between devices, padded_2(): lax.ppermute(head, axis, [((i + 1) % count, i) for i in range(count)])  14.7 us
    ppermute x4, waiting for transfers between devices, passed_along(): return lax.ppermute(value, axis, pairs)  13.4 us
    ppermute x4, starting transfers between devices, passed_along(): return lax.ppermute(value, axis, pairs)  10.6 us
    gather x4, local copies, waits for them, and re-layouts, per_device(): jnp.take_along_axis(system_vector.reshape(subs, -1), flat, axis=1)  9.71 us
  transfers between devices with their start and end apart: 12, of which 5 were waited for; matrix products, arithmetic and copies ran while one was open for 28% of the time, Pallas kernels for 0%

commit v1 on v0

v1 whole, which is shorter than its diff:
```python
import functools

import jax
import jax.numpy as jnp
from jax import lax
from jax.experimental import pallas as pl
from jax.experimental.pallas import tpu as pltpu
from jax.sharding import PartitionSpec as P

ITERS = 2
F32 = jnp.float32
BF16 = jnp.bfloat16
MESH = pl.DeviceIdType.MESH
ROOT = 0.7978845608028654
CUBE = 0.044715


def column(row):
    n = row.shape[1]
    eye = lax.broadcasted_iota(jnp.int32, (n, n), 0) == lax.broadcasted_iota(jnp.int32, (n, n), 1)
    return jnp.sum(jnp.where(eye, row, 0.0), axis=1, keepdims=True)


def lat_of(n, lats):
    return lax.broadcasted_iota(jnp.int32, (1, n), 1) % lats


def im2col(x, dst, lats):
    chans, n = x.shape
    lat = lat_of(n, lats)
    below = jnp.where(lat == 0, 0.0, pltpu.roll(x, 1, 1))
    above = jnp.where(lat == lats - 1, 0.0, pltpu.roll(x, n - 1, 1))
    for b, v in enumerate((below, x, above)):
        for a, w in enumerate((pltpu.roll(v, lats, 1), v, pltpu.roll(v, n - lats, 1))):
            at = (3 * a + b) * chans
            dst[at : at + chans, :n] = w.astype(BF16)


def stack_lons(src, lo, hi, at, dst, lats):
    feat = src.shape[0]
    n = hi - lo
    two = 2 * lats
    dst[:feat, at : at + n] = pltpu.roll(src[:, lo - two : hi], lats, 1)[:, two:].astype(BF16)
    dst[feat : 2 * feat, at : at + n] = src[:, lo:hi].astype(BF16)
    dst[2 * feat :, at : at + n] = pltpu.roll(src[:, lo : hi + two], n + two - lats, 1)[:, :n].astype(BF16)


def sum_lats(p, lats):
    chans = p.shape[0] // 3
    n = p.shape[1]
    lat = lat_of(n, lats)
    below = jnp.where(lat == 0, 0.0, pltpu.roll(p[:chans], 1, 1))
    above = jnp.where(lat == lats - 1, 0.0, pltpu.roll(p[2 * chans :], n - 1, 1))
    return p[chans : 2 * chans] + below + above


def folded(v):
    acc = v[:, :128]
    for i in range(1, v.shape[1] // 128):
        acc = acc + v[:, 128 * i : 128 * (i + 1)]
    tile = acc[:8]
    for i in range(1, acc.shape[0] // 8):
        tile = tile + acc[8 * i : 8 * (i + 1)]
    return tile


def chunks(lo, hi, size=256):
    return [(c, min(c + size, hi)) for c in range(lo, hi, size)]


def kernel(
    total, tms, lons,
    fg, bg, w1, b1, w2, b2, mw, bw, cell, chan, val, wt, step,
    out, costs,
    xe, rx, sx, sten, hf, hs, gp, qf, mx, lx, gx, ow, ov, v2, w1p, v1p, tall, wide,
    ms, mr, ar1, ar2,
    halo_send, halo_recv, m_send, m_recv, a1_send, a1_recv, a2_send, a2_recv,
):
    subs, band, chans, lats = fg.shape
    feat = w1.shape[0]
    own = band * lats
    lo, hi = 4 * lats, 4 * lats + own
    wlo, whi = 2 * lats, 6 * lats + own
    ext = hi + 4 * lats
    win = whi - wlo
    t = lax.axis_index("tm")
    l = lax.axis_index("lon")
    tp, tn = lax.rem(t + tms - 1, tms), lax.rem(t + 1, tms)
    ll, lr = lax.rem(l + lons - 1, lons), lax.rem(l + 1, lons)
    lon_peers = [lax.rem(l + d, lons) for d in range(1, lons)]
    tm_peers = [lax.rem(t + d, tms) for d in range(1, tms)]

    barrier = pltpu.get_barrier_semaphore()
    for peer in lon_peers:
        pl.semaphore_signal(barrier, inc=1, device_id=(t, peer), device_id_type=MESH)
    for peer in tm_peers:
        pl.semaphore_signal(barrier, inc=1, device_id=(peer, l), device_id_type=MESH)
    for peer in (ll, lr):
        pl.semaphore_signal(barrier, inc=1, device_id=(tn, peer), device_id_type=MESH)

    def halo_copies(it):
        src, dst = sx.at[it], rx.at[it]
        four, two = 4 * lats, 2 * lats
        first = slice(0, 1)
        parts = (
            (src.at[:, :, own - four :], dst.at[:subs, :, :lo], (t, lr)),
            (src.at[:, :, :four], dst.at[:subs, :, hi:], (t, ll)),
            (src.at[first], dst.at[subs:, :, lo:hi], (tp, l)),
            (src.at[first, :, own - two :], dst.at[subs:, :, wlo:lo], (tp, lr)),
            (src.at[first, :, :two], dst.at[subs:, :, hi:whi], (tp, ll)),
        )
        return [
            pltpu.make_async_remote_copy(
                src_ref=s, dst_ref=d, send_sem=halo_send.at[it, i], recv_sem=halo_recv.at[it, i],
                device_id=dev, device_id_type=MESH,
            )
            for i, (s, d, dev) in enumerate(parts)
        ]

    for s in range(subs):
        for i in range(0, band, 2):
            pair = jnp.concatenate([fg[s, i], fg[s, i + 1]], axis=1)
            xe[s, :, lo + i * lats : lo + (i + 2) * lats] = pair
            sx[0, s, :, i * lats : (i + 2) * lats] = pair.astype(BF16)
    pl.semaphore_wait(barrier, lons - 1 + tms - 1 + 2)
    pending = []
    halos = halo_copies(0)
    for c in halos:
        c.start()

    for a in range(3):
        for b in range(3):
            block = w2[:, (3 * a + b) * feat : (3 * a + b + 1) * feat]
            v2[b * chans : (b + 1) * chans, a * feat : (a + 1) * feat] = block
            at = (3 * (2 - a) + (2 - b)) * chans
            tall[at : at + chans, :] = block.astype(F32)
    tall[9 * chans :, :] = jnp.zeros((tall.shape[0] - 9 * chans, feat), F32)
    w1p[...] = jnp.transpose(tall[...]).astype(BF16)
    wide[:, wide.shape[1] - 128 :] = jnp.zeros((feat, 128), F32)
    wide[:, : 9 * chans] = w1[...].astype(F32)
    tall[...] = jnp.transpose(wide[...])
    for a in range(3):
        for b in range(3):
            at = (3 * (2 - a) + (2 - b)) * chans
            v1p[b * chans : (b + 1) * chans, a * feat : (a + 1) * feat] = tall[at : at + chans, :].astype(BF16)
    b1c, b2c, mwc, bwc = column(b1[...]), column(b2[...]), column(mw[...]), column(bw[...])

    fixed = jnp.zeros((), F32)
    nobs = cell.shape[1]
    for s in range(subs):
        weight, value = wt[s : s + 1, :], val[s : s + 1, :]
        fixed = fixed + jnp.sum(weight * value * value)
        at_chan = lax.broadcasted_iota(jnp.int32, (chans, nobs), 0) == chan[s : s + 1, :]
        at_cell = (lax.broadcasted_iota(jnp.int32, (own, nobs), 0) == cell[s : s + 1, :]).astype(F32).astype(BF16)
        for quantity, dst in ((weight, ow), (weight * value, ov)):
            rest, rows = quantity, []
            for _ in range(3):
                part = rest.astype(BF16).astype(F32)
                rest = rest - part
                rows.append(jnp.where(at_chan, part, 0.0).astype(BF16))
            spread = lax.dot_general(
                jnp.concatenate(rows, axis=0), at_cell, (((1,), (1,)), ((), ())), preferred_element_type=F32
            )
            dst[s] = spread[:chans] + spread[chans : 2 * chans] + spread[2 * chans :]

    starts = (t > 0).astype(F32)
    ends = (t < tms - 1).astype(F32)
    anchor = (t == 0).astype(F32)
    origin = lax.broadcasted_iota(jnp.int32, (8, 128), 0) * 128 + lax.broadcasted_iota(jnp.int32, (8, 128), 1) == 0

    alpha = None
    for it in range(ITERS):
        for c in halos:
            c.wait_recv()
        pending += halos
        for s in range(subs + 1):
            for x0, x1 in ((0, lo), (hi, ext)) if s < subs else ((wlo, whi),):
                got = rx[it, s, :, x0:x1].astype(F32)
                xe[s, :, x0:x1] = got if it == 0 else xe[s, :, x0:x1] - alpha * got

        for s in reversed(range(subs)):
            im2col(xe[s], sten, lats)
            for c0, c1 in chunks(0, ext):
                pre = jnp.dot(w1[...], sten[:, c0:c1], preferred_element_type=F32) + b1c
                sq = pre * pre
                th = jnp.tanh(ROOT * pre * (1.0 + CUBE * sq))
                half = 0.5 * (1.0 + th)
                hf[:, c0:c1] = pre * half
                slope = half + (0.5 * ROOT) * pre * (1.0 - th * th) * (1.0 + 3.0 * CUBE * sq)
                gp[s, :, c0:c1] = slope
            for c0, c1 in chunks(wlo, whi):
                stack_lons(hf, c0, c1, c0 - wlo, hs, lats)
                p = jnp.dot(v2[...], hs[:, c0 - wlo : c1 - wlo], preferred_element_type=F32)
                mx[s, :, c0 - wlo : c1 - wlo] = xe[s, :, c0:c1] + sum_lats(p, lats) + b2c
            if s == subs - 1:
                ms[it] = mx[s, :, lo - wlo : hi - wlo].astype(BF16)
                m_copy = pltpu.make_async_remote_copy(
                    src_ref=ms.at[it], dst_ref=mr.at[it], send_sem=m_send.at[it], recv_sem=m_recv.at[it],
                    device_id=(tn, l), device_id_type=MESH,
                )
                m_copy.start()
                pending.append(m_copy)

        for s in range(subs):
            scale = mwc if s < subs - 1 else mwc * ends
            lx[s + 1] = scale * (xe[s + 1, :, wlo:whi] - mx[s])

        norm = jnp.zeros((8, 128), F32)
        cost = jnp.where(origin, fixed, 0.0)
        for s in reversed(range(subs)):
            im2col(lx[s + 1], sten, lats)
            for c0, c1 in chunks(0, win):
                z = jnp.dot(w1p[:, : 9 * chans], sten[:, c0:c1], preferred_element_type=F32)
                qf[:, c0:c1] = gp[s, :, wlo + c0 : wlo + c1] * z
            pulled = []
            for c0, c1 in chunks(lo - wlo, hi - wlo):
                at = c0 - (lo - wlo)
                stack_lons(qf, c0, c1, at, hs, lats)
                p = jnp.dot(v1p[...], hs[:, at : at + c1 - c0], preferred_element_type=F32)
                pulled.append(lx[s + 1, :, c0:c1] + sum_lats(p, lats))
            pulled = jnp.concatenate(pulled, axis=1)
            x = xe[s, :, lo:hi]
            if s > 0:
                forcing = lx[s, :, lo - wlo : hi - wlo]
                defect = x - mx[s - 1, :, lo - wlo : hi - wlo]
            else:
                m_copy.wait_recv()
                defect = x - mr[it].astype(F32)
                forcing = (mwc * starts) * defect
            weighted = ow[s] * x - ov[s]
            cost = cost + folded(forcing * defect + (weighted - ov[s]) * x)
            g = forcing - pulled + weighted
            if s == 0:
                back = jnp.concatenate([bg[i] for i in range(band)], axis=1)
                departure = x - back
                pull = (bwc * anchor) * departure
                cost = cost + folded(pull * departure)
                g = g + pull
            norm = norm + folded(g * g)
            gx[s] = g
            if it < ITERS - 1:
                sx[it + 1, s] = g.astype(BF16)

        ar1[it, l, :8] = norm
        ar1[it, l, 8:] = cost
        first_phase = [
            pltpu.make_async_remote_copy(
                src_ref=ar1.at[it, l], dst_ref=ar1.at[it, l], send_sem=a1_send.at[it, i], recv_sem=a1_recv.at[it, i],
                device_id=(t, peer), device_id_type=MESH,
            )
            for i, peer in enumerate(lon_peers)
        ]
        for c in first_phase:
            c.start()
        if it < ITERS - 1:
            halos = halo_copies(it + 1)
            for c in halos:
                c.start()
        for c in first_phase:
            c.wait_recv()
        ar2[it, t] = functools.reduce(jnp.add, [ar1[it, i] for i in range(lons)])
        second_phase = [
            pltpu.make_async_remote_copy(
                src_ref=ar2.at[it, t], dst_ref=ar2.at[it, t], send_sem=a2_send.at[it, i], recv_sem=a2_recv.at[it, i],
                device_id=(peer, l), device_id_type=MESH,
            )
            for i, peer in enumerate(tm_peers)
        ]
        for c in second_phase:
            c.start()
        for c in second_phase:
            c.wait_recv()
        pending += first_phase + second_phase
        both = functools.reduce(jnp.add, [ar2[it, i] for i in range(tms)])
        costs[it] = 0.5 * jnp.sum(both[8:])
        sum_sq = jnp.sum(jnp.sum(both[:8], axis=0, keepdims=True), axis=1, keepdims=True)
        alpha = step[...] / jnp.sqrt(sum_sq / total + 1e-06)
        for s in range(subs):
            x = xe[s, :, lo:hi] - alpha * gx[s]
            if it < ITERS - 1:
                xe[s, :, lo:hi] = x
            else:
                for i in range(band):
                    out[s, i] = x[:, i * lats : (i + 1) * lats]
    for c in pending:
        c.wait_send()


def per_device(fg, bg, w1, b1, w2, b2, mw, bw, cell, chan, val, wt, step):
    subs, band, chans, lats = fg.shape
    feat = w1.shape[0]
    tms, lons = lax.axis_size("tm"), lax.axis_size("lon")
    total = float(subs * tms * band * lons * chans * lats)
    own = band * lats
    win = own + 4 * lats
    ext = own + 8 * lats
    rows = -(-9 * chans // 128) * 128
    vmem = pl.BlockSpec(memory_space=pltpu.VMEM)
    dma = pltpu.SemaphoreType.DMA
    return pl.pallas_call(
        functools.partial(kernel, total, tms, lons),
        out_shape=(
            jax.ShapeDtypeStruct(fg.shape, F32),
            jax.ShapeDtypeStruct((ITERS,), F32),
        ),
        in_specs=[vmem] * 13,
        out_specs=(vmem, pl.BlockSpec(memory_space=pltpu.SMEM)),
        scratch_shapes=[
            pltpu.VMEM((subs + 1, chans, ext), F32),
            pltpu.VMEM((ITERS, subs + 1, chans, ext), BF16),
            pltpu.VMEM((ITERS, subs, chans, own), BF16),
            pltpu.VMEM((9 * chans, ext), BF16),
            pltpu.VMEM((feat, ext), F32),
            pltpu.VMEM((3 * feat, win), BF16),
            pltpu.VMEM((subs, feat, ext), F32),
            pltpu.VMEM((feat, win), F32),
            pltpu.VMEM((subs, chans, win), F32),
            pltpu.VMEM((subs + 1, chans, win), F32),
            pltpu.VMEM((subs, chans, own), F32),
            pltpu.VMEM((subs, chans, own), F32),
            pltpu.VMEM((subs, chans, own), F32),
            pltpu.VMEM((3 * chans, 3 * feat), BF16),
            pltpu.VMEM((feat, rows), BF16),
            pltpu.VMEM((3 * chans, 3 * feat), BF16),
            pltpu.VMEM((rows, feat), F32),
            pltpu.VMEM((feat, rows), F32),
            pltpu.VMEM((ITERS, chans, own), BF16),
            pltpu.VMEM((ITERS, chans, own), BF16),
            pltpu.VMEM((ITERS, lons, 16, 128), F32),
            pltpu.VMEM((ITERS, tms, 16, 128), F32),
            dma((ITERS, 5)),
            dma((ITERS, 5)),
            dma((ITERS,)),
            dma((ITERS,)),
            dma((ITERS, lons - 1)),
            dma((ITERS, lons - 1)),
            dma((ITERS, tms - 1)),
            dma((ITERS, tms - 1)),
        ],
        compiler_params=pltpu.CompilerParams(
            collective_id=0, has_side_effects=True, vmem_limit_bytes=48 * 1024 * 1024
        ),
    )(
        fg, bg, w1, b1.reshape(1, -1), w2, b2.reshape(1, -1), mw.reshape(1, -1), bw.reshape(1, -1),
        cell, chan, val, wt, step.reshape(1, 1),
    )


def solution(mesh):
    in_specs = (
        P("tm", "lon", None, None),
        P("lon", None, None),
        P(),
        P(),
        P(),
        P(),
        P(),
        P(),
        P("tm", "lon"),
        P("tm", "lon"),
        P("tm", "lon"),
        P("tm", "lon"),
        P(),
    )
    out_specs = (P("tm", "lon", None, None), P())
    return jax.shard_map(
        per_device, mesh=mesh, in_specs=in_specs, out_specs=out_specs, check_vma=False
    )
```

time: 264 us -> 44.2 us (0.17)
  blocking collectives: 79.2 us -> 0 us
  other arithmetic: 59.8 us -> 0 us
  local copies, waits for them, and re-layouts: 53.7 us -> 4.63 us
  Pallas kernels: 0 us -> 37.9 us
  starting transfers between devices: 26 us -> 0 us
  matrix products: 19.8 us -> 0 us
  waiting for transfers between devices: 15.4 us -> 0 us
  between operations: 7.42 us -> 1.46 us
    psum x2 -> x0, blocking collectives: 79.2 us -> none  [per_device(): norm = lax.psum(squares, ('tm', 'lon'))]
    scatter-add x2 -> x0, other arithmetic: 47.2 us -> none  [per_device(): observed = jnp.zeros((subs, band * chans * lats), jnp.float32).at[rows, f...]
    pallas_call x0 -> x1, Pallas kernels: none -> 37.9 us  [per_device(): pl.pallas_call(functools.partial(kernel, total, tms, lons), out_shape=(ja...]
    ppermute x12 -> x0, starting transfers between devices: 26 us -> none  [the longest x4 14.7 us: padded_2(): lax.ppermute(head, axis, [((i + 1) % count, i) for i in range(count)])]
    dot_general x8 -> x0, matrix products: 19.8 us -> none  [convolve(): jnp.einsum('fk,snkl->snfl', weight, stacked, preferred_element_type=jnp.f...]
    concatenate x8 -> x0, local copies, waits for them, and re-layouts: 19.1 us -> none  [convolve(): jnp.concatenate([spread[:, a:a + count, :, b:b + lats] for a in range(3)...]
    ppermute x12 -> x0, waiting for transfers between devices: 15.4 us -> none  [the longest x4 13.4 us: passed_along(): return lax.ppermute(value, axis, pairs)]
    gather x4 -> x0, local copies, waits for them, and re-layouts: 9.71 us -> none  [per_device(): jnp.take_along_axis(system_vector.reshape(subs, -1), flat, axis=1)]
  transfers between devices with their start and end apart: 12 -> 0, of which waited for: 5 -> 0; matrix products, arithmetic and copies ran while one was open for 28% -> 0% of each run, Pallas kernels for 0% -> 0%
where the time goes in v1:
time: 44.2 us; the launch traced here: 44 us
  Pallas kernels  37.9 us (86%)
  local copies, waits for them, and re-layouts  4.63 us (10%)
  between operations  1.46 us (3%)
    pallas_call x1, Pallas kernels, per_device(): pl.pallas_call(functools.partial(kernel, total, tms, lons), out_shape=(ja...  37.9 us
    unnamed x26, local copies, waits for them, and re-layouts  3.6 us
    pallas_call x1, local copies, waits for them, and re-layouts, per_device(): pl.pallas_call(functools.partial(kernel, total, tms, lons), out_shape=(ja...  1.02 us

profile of v1, /device:TPU:0, one launch (start us, length us, event | category | flops | bytes accessed | tf_op | source)
XLA Modules:
  0.0 44.0 jit_solution(1575768614200478525)
XLA Ops:
  0.6 0.0 copy-start.10
  1.3 1.1 %copy.16.bg = f32[8,80,64]{2,1,0:T(8,128)S(1)} copy(f32[8,80,64]{1,2,0:T(8,128)} %param.14) | data formatting | bytes 327680 | tf_op args[1]
  2.4 0.0 copy-done.10
  2.5 0.0 copy-start.9
  2.5 0.2 copy.17.w1
  2.6 0.9 %copy-done.9 = f32[2,8,80,64]{2,3,1,0:T(8,128)S(1)} copy-done((f32[2,8,80,64]{2,3,1,0:T(8,128)S(1)}, f32[2,8,80,64]{2,3,1,0:T(8,128)}, u32[]{:S(2)}) %copy-start.9) | copy-done | bytes 327704
  3.5 0.0 copy-start
  3.5 0.0 copy-start.1
  3.5 0.0 copy-start.2
  3.5 0.0 copy-start.3
  3.5 0.0 copy-start.4
  3.5 0.0 copy-start.5
  3.5 0.0 copy-start.6
  3.5 0.0 copy-start.7
  3.6 0.0 copy-start.8
  3.6 0.2 copy.15.fg
  3.8 0.7 %copy-done = bf16[80,2304]{1,0:T(8,128)(2,1)S(1)} copy-done((bf16[80,2304]{1,0:T(8,128)(2,1)S(1)}, bf16[80,2304]{1,0:T(8,128)(2,1)}, u32[]{:S(2)}) %copy-start) | copy-done | bytes 368664
  4.5 0.0 copy-done.1
  4.5 0.0 copy-done.2
  4.5 0.0 copy-done.3
  4.5 0.0 copy-done.4
  4.5 0.0 copy-done.5
  4.5 0.0 copy-done.6
  4.5 0.0 copy-done.7
  4.5 0.0 copy-done.8
  4.5 37.9 %shard_map.140 = (f32[2,8,80,64]{3,2,1,0:T(8,128)S(1)}, f32[2]{0:T(128)S(1)}) custom-call(f32[2,8,80,64]{3,2,1,0:T(8,128)S(1)} %copy.15.fg, f32[8,80,64]{2,1,0:T(8,128)S(1)} %copy.16.bg, bf16[256,720]{1,0:T(8,128)(2,1)S(1)} %copy.17.w1, f32[1,256]{1,0:T(1,128)S(1)} %bitcast.6, bf16[80,2304]{1,0:T(8,128)(2,1)S(1)} %copy-done, f32[1,80]{1,0:T(1,128)S(1)} %bitcast.7, ...), custom_call_target="tpu_custom_call" | custom-call | tf_op jit(solution)/shard_map/pallas_call | solution.py:300
  42.5 1.0 %copy.18 = f32[2,8,80,64]{2,3,1,0:T(8,128)} copy(f32[2,8,80,64]{3,2,1,0:T(8,128)S(1)} %get-tuple-element.2) | data formatting | bytes 655360 | tf_op jit(solution)/shard_map/pallas_call | solution.py:300
  43.5 0.5 %copy.21 = f32[2]{0:T(128)} copy(f32[2]{0:T(128)S(1)} %get-tuple-element.7) | data formatting | bytes 16
Async XLA Ops:
  0.6 1.8 %copy-start.10 = (bf16[256,720]{0,1:T(8,128)(2,1)S(1)}, bf16[256,720]{0,1:T(8,128)(2,1)}, u32[]{:S(2)}) copy-start(bf16[256,720]{0,1:T(8,128)(2,1)} %param.15) | copy-start | bytes 1105924
  2.5 1.0 %copy-start.9 = (f32[2,8,80,64]{2,3,1,0:T(8,128)S(1)}, f32[2,8,80,64]{2,3,1,0:T(8,128)}, u32[]{:S(2)}) copy-start(f32[2,8,80,64]{2,3,1,0:T(8,128)} %param.13) | copy-start | bytes 983044
  3.5 1.0 %copy-start = (bf16[80,2304]{1,0:T(8,128)(2,1)S(1)}, bf16[80,2304]{1,0:T(8,128)(2,1)}, u32[]{:S(2)}) copy-start(bf16[80,2304]{1,0:T(8,128)(2,1)} %w2.1) | copy-start | bytes 1105924
  3.5 1.0 %copy-start.1 = (s32[2,256]{1,0:T(2,128)S(1)}, s32[2,256]{1,0:T(2,128)}, u32[]{:S(2)}) copy-start(s32[2,256]{1,0:T(2,128)} %cell.1) | copy-start | bytes 6148
  3.5 1.0 %copy-start.2 = (s32[2,256]{1,0:T(2,128)S(1)}, s32[2,256]{1,0:T(2,128)}, u32[]{:S(2)}) copy-start(s32[2,256]{1,0:T(2,128)} %chan.1) | copy-start | bytes 6148
  3.5 1.0 %copy-start.3 = (f32[2,256]{1,0:T(2,128)S(1)}, f32[2,256]{1,0:T(2,128)}, u32[]{:S(2)}) copy-start(f32[2,256]{1,0:T(2,128)} %val.1) | copy-start | bytes 6148
  3.5 1.0 %copy-start.4 = (f32[2,256]{1,0:T(2,128)S(1)}, f32[2,256]{1,0:T(2,128)}, u32[]{:S(2)}) copy-start(f32[2,256]{1,0:T(2,128)} %wt.1) | copy-start | bytes 6148
  3.5 1.0 %copy-start.5 = (f32[256]{0:T(256)S(1)}, f32[256]{0:T(256)}, u32[]{:S(2)}) copy-start(f32[256]{0:T(256)} %param.16) | copy-start | bytes 3076
  3.5 1.0 %copy-start.6 = (f32[80]{0:T(128)S(1)}, f32[80]{0:T(128)}, u32[]{:S(2)}) copy-start(f32[80]{0:T(128)} %param.18) | copy-start | bytes 964
  3.5 1.0 %copy-start.7 = (f32[80]{0:T(128)S(1)}, f32[80]{0:T(128)}, u32[]{:S(2)}) copy-start(f32[80]{0:T(128)} %param.19) | copy-start | bytes 964
  3.6 1.0 %copy-start.8 = (f32[80]{0:T(128)S(1)}, f32[80]{0:T(128)}, u32[]{:S(2)}) copy-start(f32[80]{0:T(128)} %param.20) | copy-start | bytes 964

commit v2 on v1

--- a/solution.py
+++ b/solution.py
@@ -30,19 +30,20 @@
     lat = lat_of(n, lats)
     below = jnp.where(lat == 0, 0.0, pltpu.roll(x, 1, 1))
     above = jnp.where(lat == lats - 1, 0.0, pltpu.roll(x, n - 1, 1))
-    for b, v in enumerate((below, x, above)):
+    for b, wide in enumerate((below, x, above)):
+        v = wide.astype(BF16)
         for a, w in enumerate((pltpu.roll(v, lats, 1), v, pltpu.roll(v, n - lats, 1))):
             at = (3 * a + b) * chans
-            dst[at : at + chans, :n] = w.astype(BF16)
+            dst[at : at + chans, :n] = w
 
 
 def stack_lons(src, lo, hi, at, dst, lats):
     feat = src.shape[0]
     n = hi - lo
     two = 2 * lats
-    dst[:feat, at : at + n] = pltpu.roll(src[:, lo - two : hi], lats, 1)[:, two:].astype(BF16)
-    dst[feat : 2 * feat, at : at + n] = src[:, lo:hi].astype(BF16)
-    dst[2 * feat :, at : at + n] = pltpu.roll(src[:, lo : hi + two], n + two - lats, 1)[:, :n].astype(BF16)
+    dst[:feat, at : at + n] = pltpu.roll(src[:, lo - two : hi], lats, 1)[:, two:]
+    dst[feat : 2 * feat, at : at + n] = src[:, lo:hi]
+    dst[2 * feat :, at : at + n] = pltpu.roll(src[:, lo : hi + two], n + two - lats, 1)[:, :n]
 
 
 def sum_lats(p, lats):
@@ -69,16 +70,15 @@
 
 
 def kernel(
-    total, tms, lons,
-    fg, bg, w1, b1, w2, b2, mw, bw, cell, chan, val, wt, step,
+    total, tms, lons, lats,
+    fg, bg, w1t, b1, w2, b2, mw, bw, cell, chan, val, wt, step,
     out, costs,
-    xe, rx, sx, sten, hf, hs, gp, qf, mx, lx, gx, ow, ov, v2, w1p, v1p, tall, wide,
+    xe, rx, sx, sten, hf, hs, gp, qf, mx, lx, gx, ow, ov, v2, w1s, w1p, v1p, tall, tall1, pp, cg,
     ms, mr, ar1, ar2,
     halo_send, halo_recv, m_send, m_recv, a1_send, a1_recv, a2_send, a2_recv,
 ):
-    subs, band, chans, lats = fg.shape
-    feat = w1.shape[0]
-    own = band * lats
+    subs, own, chans = fg.shape
+    feat = w1t.shape[1]
     lo, hi = 4 * lats, 4 * lats + own
     wlo, whi = 2 * lats, 6 * lats + own
     ext = hi + 4 * lats
@@ -118,10 +118,9 @@
         ]
 
     for s in range(subs):
-        for i in range(0, band, 2):
-            pair = jnp.concatenate([fg[s, i], fg[s, i + 1]], axis=1)
-            xe[s, :, lo + i * lats : lo + (i + 2) * lats] = pair
-            sx[0, s, :, i * lats : (i + 2) * lats] = pair.astype(BF16)
+        x = jnp.transpose(fg[s])
+        xe[s, :, lo:hi] = x
+        sx[0, s] = x.astype(BF16)
     pl.semaphore_wait(barrier, lons - 1 + tms - 1 + 2)
     pending = []
     halos = halo_copies(0)
@@ -136,13 +135,13 @@
             tall[at : at + chans, :] = block.astype(F32)
     tall[9 * chans :, :] = jnp.zeros((tall.shape[0] - 9 * chans, feat), F32)
     w1p[...] = jnp.transpose(tall[...]).astype(BF16)
-    wide[:, wide.shape[1] - 128 :] = jnp.zeros((feat, 128), F32)
-    wide[:, : 9 * chans] = w1[...].astype(F32)
-    tall[...] = jnp.transpose(wide[...])
+    tall1[: 9 * chans, :] = w1t[...].astype(F32)
+    tall1[9 * chans :, :] = jnp.zeros((tall1.shape[0] - 9 * chans, feat), F32)
+    w1s[...] = jnp.transpose(tall1[...]).astype(BF16)
     for a in range(3):
         for b in range(3):
             at = (3 * (2 - a) + (2 - b)) * chans
-            v1p[b * chans : (b + 1) * chans, a * feat : (a + 1) * feat] = tall[at : at + chans, :].astype(BF16)
+            v1p[b * chans : (b + 1) * chans, a * feat : (a + 1) * feat] = w1t[at : at + chans, :]
     b1c, b2c, mwc, bwc = column(b1[...]), column(b2[...]), column(mw[...]), column(bw[...])
 
     fixed = jnp.zeros((), F32)
@@ -170,8 +169,9 @@
 
     alpha = None
     for it in range(ITERS):
-        for c in halos:
-            c.wait_recv()
+        if it == 0:
+            for c in halos:
+                c.wait_recv()
         pending += halos
         for s in range(subs + 1):
             for x0, x1 in ((0, lo), (hi, ext)) if s < subs else ((wlo, whi),):
@@ -179,15 +179,20 @@
                 xe[s, :, x0:x1] = got if it == 0 else xe[s, :, x0:x1] - alpha * got
 
         for s in reversed(range(subs)):
-            im2col(xe[s], sten, lats)
+            if it == 0:
+                im2col(xe[s], sten, lats)
             for c0, c1 in chunks(0, ext):
-                pre = jnp.dot(w1[...], sten[:, c0:c1], preferred_element_type=F32) + b1c
+                if it == 0:
+                    pre = jnp.dot(w1s[:, : 9 * chans], sten[:, c0:c1], preferred_element_type=F32) + b1c
+                else:
+                    pre = pp[s, :, c0:c1] - alpha * cg[s, :, c0:c1]
+                if it < ITERS - 1:
+                    pp[s, :, c0:c1] = pre
                 sq = pre * pre
-                th = jnp.tanh(ROOT * pre * (1.0 + CUBE * sq))
-                half = 0.5 * (1.0 + th)
-                hf[:, c0:c1] = pre * half
-                slope = half + (0.5 * ROOT) * pre * (1.0 - th * th) * (1.0 + 3.0 * CUBE * sq)
-                gp[s, :, c0:c1] = slope
+                half = 0.5 + 0.5 * jnp.tanh(pre * (ROOT + (ROOT * CUBE) * sq))
+                hid = pre * half
+                hf[:, c0:c1] = hid.astype(BF16)
+                gp[s, :, c0:c1] = half + hid * (1.0 - half) * (2.0 * ROOT + (6.0 * ROOT * CUBE) * sq)
             for c0, c1 in chunks(wlo, whi):
                 stack_lons(hf, c0, c1, c0 - wlo, hs, lats)
                 p = jnp.dot(v2[...], hs[:, c0 - wlo : c1 - wlo], preferred_element_type=F32)
@@ -211,7 +216,7 @@
             im2col(lx[s + 1], sten, lats)
             for c0, c1 in chunks(0, win):
                 z = jnp.dot(w1p[:, : 9 * chans], sten[:, c0:c1], preferred_element_type=F32)
-                qf[:, c0:c1] = gp[s, :, wlo + c0 : wlo + c1] * z
+                qf[:, c0:c1] = (gp[s, :, wlo + c0 : wlo + c1] * z).astype(BF16)
             pulled = []
             for c0, c1 in chunks(lo - wlo, hi - wlo):
                 at = c0 - (lo - wlo)
@@ -231,7 +236,7 @@
             cost = cost + folded(forcing * defect + (weighted - ov[s]) * x)
             g = forcing - pulled + weighted
             if s == 0:
-                back = jnp.concatenate([bg[i] for i in range(band)], axis=1)
+                back = jnp.transpose(bg[...])
                 departure = x - back
                 pull = (bwc * anchor) * departure
                 cost = cost + folded(pull * departure)
@@ -268,6 +273,16 @@
         ]
         for c in second_phase:
             c.start()
+        if it < ITERS - 1:
+            for c in halos:
+                c.wait_recv()
+            for s in range(subs):
+                left, right = rx[it + 1, s, :, :lo].astype(F32), rx[it + 1, s, :, hi:].astype(F32)
+                im2col(jnp.concatenate([left, gx[s], right], axis=1), sten, lats)
+                for c0, c1 in chunks(0, ext):
+                    cg[s, :, c0:c1] = jnp.dot(
+                        w1s[:, : 9 * chans], sten[:, c0:c1], preferred_element_type=F32
+                    )
         for c in second_phase:
             c.wait_recv()
         pending += first_phase + second_phase
@@ -280,8 +295,7 @@
             if it < ITERS - 1:
                 xe[s, :, lo:hi] = x
             else:
-                for i in range(band):
-                    out[s, i] = x[:, i * lats : (i + 1) * lats]
+                out[s] = jnp.transpose(x)
     for c in pending:
         c.wait_send()
 
@@ -297,10 +311,10 @@
     rows = -(-9 * chans // 128) * 128
     vmem = pl.BlockSpec(memory_space=pltpu.VMEM)
     dma = pltpu.SemaphoreType.DMA
-    return pl.pallas_call(
-        functools.partial(kernel, total, tms, lons),
+    analysis, costs = pl.pallas_call(
+        functools.partial(kernel, total, tms, lons, lats),
         out_shape=(
-            jax.ShapeDtypeStruct(fg.shape, F32),
+            jax.ShapeDtypeStruct((subs, own, chans), F32),
             jax.ShapeDtypeStruct((ITERS,), F32),
         ),
         in_specs=[vmem] * 13,
@@ -310,10 +324,10 @@
             pltpu.VMEM((ITERS, subs + 1, chans, ext), BF16),
             pltpu.VMEM((ITERS, subs, chans, own), BF16),
             pltpu.VMEM((9 * chans, ext), BF16),
-            pltpu.VMEM((feat, ext), F32),
+            pltpu.VMEM((feat, ext), BF16),
             pltpu.VMEM((3 * feat, win), BF16),
             pltpu.VMEM((subs, feat, ext), F32),
-            pltpu.VMEM((feat, win), F32),
+            pltpu.VMEM((feat, win), BF16),
             pltpu.VMEM((subs, chans, win), F32),
             pltpu.VMEM((subs + 1, chans, win), F32),
             pltpu.VMEM((subs, chans, own), F32),
@@ -321,9 +335,12 @@
             pltpu.VMEM((subs, chans, own), F32),
             pltpu.VMEM((3 * chans, 3 * feat), BF16),
             pltpu.VMEM((feat, rows), BF16),
+            pltpu.VMEM((feat, rows), BF16),
             pltpu.VMEM((3 * chans, 3 * feat), BF16),
             pltpu.VMEM((rows, feat), F32),
-            pltpu.VMEM((feat, rows), F32),
+            pltpu.VMEM((rows, feat), F32),
+            pltpu.VMEM((subs, feat, ext), F32),
+            pltpu.VMEM((subs, feat, ext), F32),
             pltpu.VMEM((ITERS, chans, own), BF16),
             pltpu.VMEM((ITERS, chans, own), BF16),
             pltpu.VMEM((ITERS, lons, 16, 128), F32),
@@ -341,9 +358,10 @@
             collective_id=0, has_side_effects=True, vmem_limit_bytes=48 * 1024 * 1024
         ),
     )(
-        fg, bg, w1, b1.reshape(1, -1), w2, b2.reshape(1, -1), mw.reshape(1, -1), bw.reshape(1, -1),
+        jnp.swapaxes(fg, 2, 3).reshape(subs, own, chans), jnp.swapaxes(bg, 1, 2).reshape(own, chans), w1.T, b1.reshape(1, -1), w2, b2.reshape(1, -1), mw.reshape(1, -1), bw.reshape(1, -1),
         cell, chan, val, wt, step.reshape(1, 1),
     )
+    return jnp.swapaxes(analysis.reshape(subs, band, lats, chans), 2, 3), costs
 
 
 def solution(mesh):

time: 44.2 us -> 45.3 us (1.025)
  local copies, waits for them, and re-layouts: 4.63 us -> 5.99 us
    unnamed x26, local copies, waits for them, and re-layouts: 3.6 us -> 5.99 us
    pallas_call x1 -> x0, local copies, waits for them, and re-layouts: 1.02 us -> none  [per_device(): pl.pallas_call(functools.partial(kernel, total, tms, lons), out_shape=(ja...]
where the time goes in v2:
time: 45.3 us; the launch traced here: 45 us
  Pallas kernels  37.7 us (83%)
  local copies, waits for them, and re-layouts  5.99 us (13%)
  between operations  1.36 us (3%)
    pallas_call x1, Pallas kernels, per_device(): pl.pallas_call(functools.partial(kernel, total, tms, lons, lats), out_sha...  37.7 us
    unnamed x26, local copies, waits for them, and re-layouts  5.99 us

profile of v2, /device:TPU:0, one launch (start us, length us, event | category | flops | bytes accessed | tf_op | source)
XLA Modules:
  0.0 45.0 jit_solution(8947111065324123862)
XLA Ops:
  1.3 0.0 copy-start.9
  1.3 0.0 copy-start.10
  1.3 0.0 copy-start.11
  1.3 0.0 copy-start.7
  1.3 0.0 copy-start.6
  1.3 0.0 copy-start.5
  1.3 0.0 copy-start.4
  1.4 0.0 copy-start.8
  1.4 0.6 %copy-done.9 = f32[80]{0:T(128)S(1)} copy-done((f32[80]{0:T(128)S(1)}, f32[80]{0:T(128)}, u32[]{:S(2)}) %copy-start.9) | copy-done | bytes 344
  1.9 0.0 copy-done.10
  2.0 0.0 copy-done.11
  2.0 0.0 copy-done.7
  2.0 0.0 copy-done.6
  2.0 0.0 copy-done.5
  2.0 0.0 copy-done.4
  2.1 0.0 copy-done.8
  2.1 0.0 copy-start
  2.1 1.0 %copy-done = f32[2,8,80,64]{2,3,1,0:T(8,128)S(1)} copy-done((f32[2,8,80,64]{2,3,1,0:T(8,128)S(1)}, f32[2,8,80,64]{2,3,1,0:T(8,128)}, u32[]{:S(2)}) %copy-start) | copy-done | bytes 327704
  3.1 0.0 copy-start.1
  3.1 1.0 %copy-done.1 = bf16[256,720]{0,1:T(8,128)(2,1)S(1)} copy-done((bf16[256,720]{0,1:T(8,128)(2,1)S(1)}, bf16[256,720]{0,1:T(8,128)(2,1)}, u32[]{:S(2)}) %copy-start.1) | copy-done | bytes 368664
  4.1 0.0 copy-start.2
  4.1 1.0 %copy-done.2 = bf16[80,2304]{1,0:T(8,128)(2,1)S(1)} copy-done((bf16[80,2304]{1,0:T(8,128)(2,1)S(1)}, bf16[80,2304]{1,0:T(8,128)(2,1)}, u32[]{:S(2)}) %copy-start.2) | copy-done | bytes 368664
  5.1 0.0 copy-start.3
  5.1 0.9 %copy-done.3 = f32[8,80,64]{1,2,0:T(8,128)S(1)} copy-done((f32[8,80,64]{1,2,0:T(8,128)S(1)}, f32[8,80,64]{1,2,0:T(8,128)}, u32[]{:S(2)}) %copy-start.3) | copy-done | bytes 163864
  6.0 37.7 %shard_map.140 = (f32[2,512,80]{2,1,0:T(8,128)S(1)}, f32[2]{0:T(128)S(1)}) custom-call(f32[2,512,80]{2,1,0:T(8,128)S(1)} %bitcast.16, f32[512,80]{1,0:T(8,128)S(1)} %bitcast.19, bf16[720,256]{1,0:T(8,128)(2,1)S(1)} %bitcast.18, f32[1,256]{1,0:T(1,128)S(1)} %bitcast.20, bf16[80,2304]{1,0:T(8,128)(2,1)S(1)} %copy-done.2, f32[1,80]{1,0:T(1,128)S(1)} %bitcast.21, ...), custom_call_target="tpu_custom_call" | custom-call | tf_op jit(solution)/shard_map/pallas_call | solution.py:314
  43.7 0.8 %copy.18 = f32[2,8,80,64]{2,3,1,0:T(8,128)} copy(f32[2,8,80,64]{2,3,1,0:T(8,128)S(1)} %bitcast.17) | data formatting | bytes 655360
  44.5 0.5 %copy.19 = f32[2]{0:T(128)} copy(f32[2]{0:T(128)S(1)} %get-tuple-element.9) | data formatting | bytes 16
Async XLA Ops:
  1.3 0.7 %copy-start.9 = (f32[80]{0:T(128)S(1)}, f32[80]{0:T(128)}, u32[]{:S(2)}) copy-start(f32[80]{0:T(128)} %param.18) | copy-start | bytes 964
  1.3 0.7 %copy-start.10 = (f32[80]{0:T(128)S(1)}, f32[80]{0:T(128)}, u32[]{:S(2)}) copy-start(f32[80]{0:T(128)} %param.19) | copy-start | bytes 964
  1.3 0.7 %copy-start.11 = (f32[80]{0:T(128)S(1)}, f32[80]{0:T(128)}, u32[]{:S(2)}) copy-start(f32[80]{0:T(128)} %param.20) | copy-start | bytes 964
  1.3 0.7 %copy-start.7 = (f32[2,256]{1,0:T(2,128)S(1)}, f32[2,256]{1,0:T(2,128)}, u32[]{:S(2)}) copy-start(f32[2,256]{1,0:T(2,128)} %wt.1) | copy-start | bytes 6148
  1.3 0.7 %copy-start.6 = (f32[2,256]{1,0:T(2,128)S(1)}, f32[2,256]{1,0:T(2,128)}, u32[]{:S(2)}) copy-start(f32[2,256]{1,0:T(2,128)} %val.1) | copy-start | bytes 6148
  1.3 0.7 %copy-start.5 = (s32[2,256]{1,0:T(2,128)S(1)}, s32[2,256]{1,0:T(2,128)}, u32[]{:S(2)}) copy-start(s32[2,256]{1,0:T(2,128)} %chan.1) | copy-start | bytes 6148
  1.3 0.7 %copy-start.4 = (s32[2,256]{1,0:T(2,128)S(1)}, s32[2,256]{1,0:T(2,128)}, u32[]{:S(2)}) copy-start(s32[2,256]{1,0:T(2,128)} %cell.1) | copy-start | bytes 6148
  1.4 0.7 %copy-start.8 = (f32[256]{0:T(256)S(1)}, f32[256]{0:T(256)}, u32[]{:S(2)}) copy-start(f32[256]{0:T(256)} %param.16) | copy-start | bytes 3076
  2.1 1.0 %copy-start = (f32[2,8,80,64]{2,3,1,0:T(8,128)S(1)}, f32[2,8,80,64]{2,3,1,0:T(8,128)}, u32[]{:S(2)}) copy-start(f32[2,8,80,64]{2,3,1,0:T(8,128)} %param.13) | copy-start | bytes 983044
  3.1 1.0 %copy-start.1 = (bf16[256,720]{0,1:T(8,128)(2,1)S(1)}, bf16[256,720]{0,1:T(8,128)(2,1)}, u32[]{:S(2)}) copy-start(bf16[256,720]{0,1:T(8,128)(2,1)} %param.15) | copy-start | bytes 1105924
  4.1 1.0 %copy-start.2 = (bf16[80,2304]{1,0:T(8,128)(2,1)S(1)}, bf16[80,2304]{1,0:T(8,128)(2,1)}, u32[]{:S(2)}) copy-start(bf16[80,2304]{1,0:T(8,128)(2,1)} %w2.1) | copy-start | bytes 1105924
  5.1 0.9 %copy-start.3 = (f32[8,80,64]{1,2,0:T(8,128)S(1)}, f32[8,80,64]{1,2,0:T(8,128)}, u32[]{:S(2)}) copy-start(f32[8,80,64]{1,2,0:T(8,128)} %param.14) | copy-start | bytes 491524

commit v3 on v2

--- a/solution.py
+++ b/solution.py
@@ -71,18 +71,23 @@
 
 def kernel(
     total, tms, lons, lats,
-    fg, bg, w1t, b1, w2, b2, mw, bw, cell, chan, val, wt, step,
-    out, costs,
-    xe, rx, sx, sten, hf, hs, gp, qf, mx, lx, gx, ow, ov, v2, w1s, w1p, v1p, tall, tall1, pp, cg,
-    ms, mr, ar1, ar2,
-    halo_send, halo_recv, m_send, m_recv, a1_send, a1_recv, a2_send, a2_recv,
+    *refs,
 ):
+    sources, step, out, costs = refs[:12], refs[12], refs[13], refs[14]
+    fg, bg, w1t, b1, w2, b2, mw, bw, cell, chan, val, wt = held = refs[15:27]
+    (
+        xe, rx, sx, sten, hf, hs, gp, qf, mx, lx, gx, ow, ov, v2, w1s, w1p, v1p, tall, tall1, pp, cg,
+        ms, mr, ls, le, ar1, ar2,
+        in_sem, halo_send, halo_recv, edge_send, edge_recv, m_send, m_recv, a1_send, a1_recv, a2_send, a2_recv,
+    ) = refs[27:]
     subs, own, chans = fg.shape
     feat = w1t.shape[1]
-    lo, hi = 4 * lats, 4 * lats + own
-    wlo, whi = 2 * lats, 6 * lats + own
-    ext = hi + 4 * lats
-    win = whi - wlo
+    two = 2 * lats
+    lo, hi = two, two + own
+    ext = hi + two
+    loads = [pltpu.make_async_copy(src, dst, in_sem.at[i]) for i, (src, dst) in enumerate(zip(sources, held))]
+    for c in loads:
+        c.start()
     t = lax.axis_index("tm")
     l = lax.axis_index("lon")
     tp, tn = lax.rem(t + tms - 1, tms), lax.rem(t + 1, tms)
@@ -95,19 +100,13 @@
         pl.semaphore_signal(barrier, inc=1, device_id=(t, peer), device_id_type=MESH)
     for peer in tm_peers:
         pl.semaphore_signal(barrier, inc=1, device_id=(peer, l), device_id_type=MESH)
-    for peer in (ll, lr):
-        pl.semaphore_signal(barrier, inc=1, device_id=(tn, peer), device_id_type=MESH)
 
     def halo_copies(it):
         src, dst = sx.at[it], rx.at[it]
-        four, two = 4 * lats, 2 * lats
-        first = slice(0, 1)
         parts = (
-            (src.at[:, :, own - four :], dst.at[:subs, :, :lo], (t, lr)),
-            (src.at[:, :, :four], dst.at[:subs, :, hi:], (t, ll)),
-            (src.at[first], dst.at[subs:, :, lo:hi], (tp, l)),
-            (src.at[first, :, own - two :], dst.at[subs:, :, wlo:lo], (tp, lr)),
-            (src.at[first, :, :two], dst.at[subs:, :, hi:whi], (tp, ll)),
+            (src.at[:, :, own - two :], dst.at[:subs, :, :lo], (t, lr)),
+            (src.at[:, :, :two], dst.at[:subs, :, hi:], (t, ll)),
+            (src.at[:1], dst.at[subs:, :, lo:hi], (tp, l)),
         )
         return [
             pltpu.make_async_remote_copy(
@@ -117,15 +116,30 @@
             for i, (s, d, dev) in enumerate(parts)
         ]
 
+    def edge_copies(it, s):
+        parts = ((slice(own - two, own), slice(0, lo), lr), (slice(0, two), slice(hi, ext), ll))
+        return [
+            pltpu.make_async_remote_copy(
+                src_ref=ls.at[it, s, :, x], dst_ref=le.at[it, s, :, y],
+                send_sem=edge_send.at[it, s, i], recv_sem=edge_recv.at[it, s, i],
+                device_id=(t, peer), device_id_type=MESH,
+            )
+            for i, (x, y, peer) in enumerate(parts)
+        ]
+
+    loads[0].wait()
     for s in range(subs):
         x = jnp.transpose(fg[s])
         xe[s, :, lo:hi] = x
         sx[0, s] = x.astype(BF16)
-    pl.semaphore_wait(barrier, lons - 1 + tms - 1 + 2)
+    pl.semaphore_wait(barrier, lons - 1 + tms - 1)
     pending = []
     halos = halo_copies(0)
     for c in halos:
         c.start()
+
+    for c in loads[1:]:
+        c.wait()
 
     for a in range(3):
         for b in range(3):
@@ -151,16 +165,18 @@
         fixed = fixed + jnp.sum(weight * value * value)
         at_chan = lax.broadcasted_iota(jnp.int32, (chans, nobs), 0) == chan[s : s + 1, :]
         at_cell = (lax.broadcasted_iota(jnp.int32, (own, nobs), 0) == cell[s : s + 1, :]).astype(F32).astype(BF16)
-        for quantity, dst in ((weight, ow), (weight * value, ov)):
-            rest, rows = quantity, []
+        rows = []
+        for rest in (weight, weight * value):
             for _ in range(3):
                 part = rest.astype(BF16).astype(F32)
                 rest = rest - part
                 rows.append(jnp.where(at_chan, part, 0.0).astype(BF16))
-            spread = lax.dot_general(
-                jnp.concatenate(rows, axis=0), at_cell, (((1,), (1,)), ((), ())), preferred_element_type=F32
-            )
-            dst[s] = spread[:chans] + spread[chans : 2 * chans] + spread[2 * chans :]
+        spread = lax.dot_general(
+            jnp.concatenate(rows, axis=0), at_cell, (((1,), (1,)), ((), ())), preferred_element_type=F32
+        )
+        spread = [spread[i * chans : (i + 1) * chans] for i in range(6)]
+        ow[s] = spread[0] + spread[1] + spread[2]
+        ov[s] = spread[3] + spread[4] + spread[5]
 
     starts = (t > 0).astype(F32)
     ends = (t < tms - 1).astype(F32)
@@ -174,10 +190,11 @@
                 c.wait_recv()
         pending += halos
         for s in range(subs + 1):
-            for x0, x1 in ((0, lo), (hi, ext)) if s < subs else ((wlo, whi),):
+            for x0, x1 in ((0, lo), (hi, ext)) if s < subs else ((lo, hi),):
                 got = rx[it, s, :, x0:x1].astype(F32)
                 xe[s, :, x0:x1] = got if it == 0 else xe[s, :, x0:x1] - alpha * got
 
+        edges = {}
         for s in reversed(range(subs)):
             if it == 0:
                 im2col(xe[s], sten, lats)
@@ -193,12 +210,13 @@
                 hid = pre * half
                 hf[:, c0:c1] = hid.astype(BF16)
                 gp[s, :, c0:c1] = half + hid * (1.0 - half) * (2.0 * ROOT + (6.0 * ROOT * CUBE) * sq)
-            for c0, c1 in chunks(wlo, whi):
-                stack_lons(hf, c0, c1, c0 - wlo, hs, lats)
-                p = jnp.dot(v2[...], hs[:, c0 - wlo : c1 - wlo], preferred_element_type=F32)
-                mx[s, :, c0 - wlo : c1 - wlo] = xe[s, :, c0:c1] + sum_lats(p, lats) + b2c
+            for c0, c1 in chunks(lo, hi):
+                at = c0 - lo
+                stack_lons(hf, c0, c1, at, hs, lats)
+                p = jnp.dot(v2[...], hs[:, at : at + c1 - c0], preferred_element_type=F32)
+                mx[s, :, at : at + c1 - c0] = xe[s, :, c0:c1] + sum_lats(p, lats) + b2c
             if s == subs - 1:
-                ms[it] = mx[s, :, lo - wlo : hi - wlo].astype(BF16)
+                ms[it] = mx[s].astype(BF16)
                 m_copy = pltpu.make_async_remote_copy(
                     src_ref=ms.at[it], dst_ref=mr.at[it], send_sem=m_send.at[it], recv_sem=m_recv.at[it],
                     device_id=(tn, l), device_id_type=MESH,
@@ -206,28 +224,36 @@
                 m_copy.start()
                 pending.append(m_copy)
 
-        for s in range(subs):
-            scale = mwc if s < subs - 1 else mwc * ends
-            lx[s + 1] = scale * (xe[s + 1, :, wlo:whi] - mx[s])
+            forcing = (mwc if s < subs - 1 else mwc * ends) * (xe[s + 1, :, lo:hi] - mx[s])
+            lx[s + 1, :, lo:hi] = forcing
+            ls[it, s] = forcing.astype(BF16)
+            edges[s] = edge_copies(it, s)
+            for c in edges[s]:
+                c.start()
+            pending += edges[s]
 
         norm = jnp.zeros((8, 128), F32)
         cost = jnp.where(origin, fixed, 0.0)
         for s in reversed(range(subs)):
+            for c in edges[s]:
+                c.wait_recv()
+            lx[s + 1, :, :lo] = le[it, s, :, :lo].astype(F32)
+            lx[s + 1, :, hi:] = le[it, s, :, hi:].astype(F32)
             im2col(lx[s + 1], sten, lats)
-            for c0, c1 in chunks(0, win):
+            for c0, c1 in chunks(0, ext):
                 z = jnp.dot(w1p[:, : 9 * chans], sten[:, c0:c1], preferred_element_type=F32)
-                qf[:, c0:c1] = (gp[s, :, wlo + c0 : wlo + c1] * z).astype(BF16)
+                qf[:, c0:c1] = (gp[s, :, c0:c1] * z).astype(BF16)
             pulled = []
-            for c0, c1 in chunks(lo - wlo, hi - wlo):
-                at = c0 - (lo - wlo)
+            for c0, c1 in chunks(lo, hi):
+                at = c0 - lo
                 stack_lons(qf, c0, c1, at, hs, lats)
                 p = jnp.dot(v1p[...], hs[:, at : at + c1 - c0], preferred_element_type=F32)
                 pulled.append(lx[s + 1, :, c0:c1] + sum_lats(p, lats))
             pulled = jnp.concatenate(pulled, axis=1)
             x = xe[s, :, lo:hi]
             if s > 0:
-                forcing = lx[s, :, lo - wlo : hi - wlo]
-                defect = x - mx[s - 1, :, lo - wlo : hi - wlo]
+                forcing = lx[s, :, lo:hi]
+                defect = x - mx[s - 1]
             else:
                 m_copy.wait_recv()
                 defect = x - mr[it].astype(F32)
@@ -306,30 +332,35 @@
     tms, lons = lax.axis_size("tm"), lax.axis_size("lon")
     total = float(subs * tms * band * lons * chans * lats)
     own = band * lats
-    win = own + 4 * lats
-    ext = own + 8 * lats
+    ext = own + 4 * lats
     rows = -(-9 * chans // 128) * 128
     vmem = pl.BlockSpec(memory_space=pltpu.VMEM)
     dma = pltpu.SemaphoreType.DMA
+    arrays = (
+        jnp.swapaxes(fg, 2, 3).reshape(subs, own, chans), jnp.swapaxes(bg, 1, 2).reshape(own, chans),
+        w1.T, b1.reshape(1, -1), w2, b2.reshape(1, -1), mw.reshape(1, -1), bw.reshape(1, -1),
+        cell, chan, val, wt,
+    )
     analysis, costs = pl.pallas_call(
         functools.partial(kernel, total, tms, lons, lats),
         out_shape=(
             jax.ShapeDtypeStruct((subs, own, chans), F32),
             jax.ShapeDtypeStruct((ITERS,), F32),
         ),
-        in_specs=[vmem] * 13,
+        in_specs=[pl.BlockSpec(memory_space=pl.ANY)] * 12 + [vmem],
         out_specs=(vmem, pl.BlockSpec(memory_space=pltpu.SMEM)),
-        scratch_shapes=[
+        scratch_shapes=[pltpu.VMEM(v.shape, v.dtype) for v in arrays]
+        + [
             pltpu.VMEM((subs + 1, chans, ext), F32),
             pltpu.VMEM((ITERS, subs + 1, chans, ext), BF16),
             pltpu.VMEM((ITERS, subs, chans, own), BF16),
             pltpu.VMEM((9 * chans, ext), BF16),
             pltpu.VMEM((feat, ext), BF16),
-            pltpu.VMEM((3 * feat, win), BF16),
+            pltpu.VMEM((3 * feat, own), BF16),
             pltpu.VMEM((subs, feat, ext), F32),
-            pltpu.VMEM((feat, win), BF16),
-            pltpu.VMEM((subs, chans, win), F32),
-            pltpu.VMEM((subs + 1, chans, win), F32),
+            pltpu.VMEM((feat, ext), BF16),
+            pltpu.VMEM((subs, chans, own), F32),
+            pltpu.VMEM((subs + 1, chans, ext), F32),
             pltpu.VMEM((subs, chans, own), F32),
             pltpu.VMEM((subs, chans, own), F32),
             pltpu.VMEM((subs, chans, own), F32),
@@ -343,10 +374,15 @@
             pltpu.VMEM((subs, feat, ext), F32),
             pltpu.VMEM((ITERS, chans, own), BF16),
             pltpu.VMEM((ITERS, chans, own), BF16),
+            pltpu.VMEM((ITERS, subs, chans, own), BF16),
+            pltpu.VMEM((ITERS, subs, chans, ext), BF16),
             pltpu.VMEM((ITERS, lons, 16, 128), F32),
             pltpu.VMEM((ITERS, tms, 16, 128), F32),
-            dma((ITERS, 5)),
-            dma((ITERS, 5)),
+            dma((12,)),
+            dma((ITERS, 3)),
+            dma((ITERS, 3)),
+            dma((ITERS, subs, 2)),
+            dma((ITERS, subs, 2)),
             dma((ITERS,)),
             dma((ITERS,)),
             dma((ITERS, lons - 1)),
@@ -355,12 +391,9 @@
             dma((ITERS, tms - 1)),
         ],
         compiler_params=pltpu.CompilerParams(
-            collective_id=0, has_side_effects=True, vmem_limit_bytes=48 * 1024 * 1024
+            collective_id=0, has_side_effects=True, vmem_limit_bytes=60 * 1024 * 1024
         ),
-    )(
-        jnp.swapaxes(fg, 2, 3).reshape(subs, own, chans), jnp.swapaxes(bg, 1, 2).reshape(own, chans), w1.T, b1.reshape(1, -1), w2, b2.reshape(1, -1), mw.reshape(1, -1), bw.reshape(1, -1),
-        cell, chan, val, wt, step.reshape(1, 1),
-    )
+    )(*arrays, step.reshape(1, 1))
     return jnp.swapaxes(analysis.reshape(subs, band, lats, chans), 2, 3), costs
 
 

time: 45.3 us -> 43 us (0.949)
  local copies, waits for them, and re-layouts: 5.99 us -> 2.4 us
  Pallas kernels: 37.7 us -> 39.2 us
    unnamed x26 -> x4, local copies, waits for them, and re-layouts: 5.99 us -> 2.4 us
    pallas_call x1, Pallas kernels: 37.7 us -> 39.2 us  [per_device(): pl.pallas_call(functools.partial(kernel, total, tms, lons, lats), out_sha...]
where the time goes in v3:
time: 43 us; the launch traced here: 42.9 us
  Pallas kernels  39.2 us (91%)
  local copies, waits for them, and re-layouts  2.4 us (6%)
  between operations  1.3 us (3%)
    pallas_call x1, Pallas kernels, per_device(): pl.pallas_call(functools.partial(kernel, total, tms, lons, lats), out_sha...  39.2 us
    unnamed x4, local copies, waits for them, and re-layouts  2.4 us

profile of v3, /device:TPU:0, one launch (start us, length us, event | category | flops | bytes accessed | tf_op | source)
XLA Modules:
  0.0 42.9 jit_solution(13916484775392680634)
XLA Ops:
  1.3 39.2 %shard_map.140 = (f32[2,512,80]{2,1,0:T(8,128)}, f32[2]{0:T(128)}) custom-call(f32[2,512,80]{2,1,0:T(8,128)} %bitcast.16, f32[512,80]{1,0:T(8,128)} %bitcast.19, bf16[720,256]{1,0:T(8,128)(2,1)} %bitcast.18, f32[1,256]{1,0:T(1,128)} %bitcast.20, bf16[80,2304]{1,0:T(8,128)(2,1)} %refs_4_.1, f32[1,80]{1,0:T(1,128)} %bitcast.21, f32[1,80]{1,0:T(1,128)} %bitcast.22, ...), custom_call_target="tpu_custom_call" | custom-call | tf_op jit(solution)/shard_map/pallas_call | solution.py:344
  40.5 0.0 copy-start
  40.5 1.9 %copy.18 = f32[2,8,80,64]{2,3,1,0:T(8,128)} copy(f32[2,8,80,64]{2,3,1,0:T(8,128)} %bitcast.17) | data formatting | bytes 655360
  42.4 0.0 copy-done
  42.4 0.5 %copy.19 = f32[2]{0:T(128)} copy(f32[2]{0:T(128)S(1)} %copy-done) | data formatting | bytes 16
Async XLA Ops:
  40.5 1.9 %copy-start = (f32[2]{0:T(128)S(1)}, f32[2]{0:T(128)}, u32[]{:S(2)}) copy-start(f32[2]{0:T(128)} %get-tuple-element.9) | copy-start | bytes 28

commit v4 on v3

--- a/solution.py
+++ b/solution.py
@@ -272,8 +272,10 @@
             if it < ITERS - 1:
                 sx[it + 1, s] = g.astype(BF16)
 
-        ar1[it, l, :8] = norm
-        ar1[it, l, 8:] = cost
+        norm, cost = jnp.sum(norm, axis=0, keepdims=True), jnp.sum(cost, axis=0, keepdims=True)
+        low = lax.broadcasted_iota(jnp.int32, (1, 128), 1) < 64
+        fold = lambda v: v + jnp.concatenate([v[:, 64:], v[:, :64]], axis=1)
+        ar1[it, l] = jnp.where(low, fold(norm), fold(cost))
         first_phase = [
             pltpu.make_async_remote_copy(
                 src_ref=ar1.at[it, l], dst_ref=ar1.at[it, l], send_sem=a1_send.at[it, i], recv_sem=a1_recv.at[it, i],
@@ -313,8 +315,8 @@
             c.wait_recv()
         pending += first_phase + second_phase
         both = functools.reduce(jnp.add, [ar2[it, i] for i in range(tms)])
-        costs[it] = 0.5 * jnp.sum(both[8:])
-        sum_sq = jnp.sum(jnp.sum(both[:8], axis=0, keepdims=True), axis=1, keepdims=True)
+        costs[it] = 0.5 * jnp.sum(jnp.where(low, 0.0, both))
+        sum_sq = jnp.sum(jnp.where(low, both, 0.0), axis=1, keepdims=True)
         alpha = step[...] / jnp.sqrt(sum_sq / total + 1e-06)
         for s in range(subs):
             x = xe[s, :, lo:hi] - alpha * gx[s]
@@ -376,8 +378,8 @@
             pltpu.VMEM((ITERS, chans, own), BF16),
             pltpu.VMEM((ITERS, subs, chans, own), BF16),
             pltpu.VMEM((ITERS, subs, chans, ext), BF16),
-            pltpu.VMEM((ITERS, lons, 16, 128), F32),
-            pltpu.VMEM((ITERS, tms, 16, 128), F32),
+            pltpu.VMEM((ITERS, lons, 1, 128), F32),
+            pltpu.VMEM((ITERS, tms, 1, 128), F32),
             dma((12,)),
             dma((ITERS, 3)),
             dma((ITERS, 3)),

time: 43 us -> 42.6 us (level)
  Pallas kernels: 39.2 us -> 38.7 us
    pallas_call x1, Pallas kernels: 39.2 us -> 38.7 us  [per_device(): pl.pallas_call(functools.partial(kernel, total, tms, lons, lats), out_sha...]
where the time goes in v4:
time: 42.6 us; the launch traced here: 42.4 us
  Pallas kernels  38.7 us (91%)
  local copies, waits for them, and re-layouts  2.4 us (6%)
  between operations  1.3 us (3%)
    pallas_call x1, Pallas kernels, per_device(): pl.pallas_call(functools.partial(kernel, total, tms, lons, lats), out_sha...  38.7 us
    unnamed x4, local copies, waits for them, and re-layouts  2.4 us

profile of v4, /device:TPU:0, one launch (start us, length us, event | category | flops | bytes accessed | tf_op | source)
XLA Modules:
  0.0 42.4 jit_solution(15246152736133116190)
XLA Ops:
  1.3 38.7 %shard_map.140 = (f32[2,512,80]{2,1,0:T(8,128)}, f32[2]{0:T(128)}) custom-call(f32[2,512,80]{2,1,0:T(8,128)} %bitcast.16, f32[512,80]{1,0:T(8,128)} %bitcast.19, bf16[720,256]{1,0:T(8,128)(2,1)} %bitcast.18, f32[1,256]{1,0:T(1,128)} %bitcast.20, bf16[80,2304]{1,0:T(8,128)(2,1)} %refs_4_.1, f32[1,80]{1,0:T(1,128)} %bitcast.21, f32[1,80]{1,0:T(1,128)} %bitcast.22, ...), custom_call_target="tpu_custom_call" | custom-call | tf_op jit(solution)/shard_map/pallas_call | solution.py:346
  40.0 0.0 copy-start
  40.0 1.9 %copy.18 = f32[2,8,80,64]{2,3,1,0:T(8,128)} copy(f32[2,8,80,64]{2,3,1,0:T(8,128)} %bitcast.17) | data formatting | bytes 655360
  41.9 0.0 copy-done
  41.9 0.5 %copy.19 = f32[2]{0:T(128)} copy(f32[2]{0:T(128)S(1)} %copy-done) | data formatting | bytes 16
Async XLA Ops:
  40.0 1.9 %copy-start = (f32[2]{0:T(128)S(1)}, f32[2]{0:T(128)}, u32[]{:S(2)}) copy-start(f32[2]{0:T(128)} %get-tuple-element.9) | copy-start | bytes 28
